TPU v7x, 1024 devices: a whole 4x4x32 slice. The times are simulated.
1024 devices in a mesh: grp: 16 (over y, x), bal: 64 (over z, core).
Axes of the slice: x: 4, y: 4, z: 32, core: 2. Of those that a mesh axis runs over, the one named last changes fastest.
Arguments:
- tracers: float32 [2, 64, 64, 16384], P(None, None, 'grp', 'bal'), may hold values from -6 to 6
- winds: bfloat16 [2, 64, 64, 16384], P(None, None, 'grp', 'bal'), may hold values from -16 to 16
- node_mass: float32 [64, 16384], P('grp', 'bal'), may hold values from 0.07 to 5.6
- column_cost: int32 [32, 8192], P('grp', 'bal'), may hold values from 1 to 3, as said below
- weight_in: bfloat16 [256, 1024], replicated, may hold values from -0.375 to 0.375
- weight_out: bfloat16 [1024, 256], replicated, may hold values from -0.1875 to 0.1875
Outputs:
- tracers_next: float32 [2, 64, 64, 16384], P(None, None, 'grp', 'bal')
- columns_out: bfloat16 [4, 64, 32, 8192], P(None, None, 'grp', 'bal')
Inputs may be any that keep to these rules, and one draw needn't show every extreme that they name: `column_cost`: among the columns of one index of grp (rows 2 * g to 2 * g + 1 of all columns), exactly a quarter have cost 3 and exactly a quarter cost 2.
All inputs are finite; a program needn't handle non-finite values.
Results may differ from a plain program's by a relative error of at most 0.008.
Values may be sent and summed in bfloat16 or wider, within the bound.
No kernel may reach another device: no remote copies, remote signals or barrier semaphores. Data moves between devices by JAX's collectives and lax.ppermute only.
A program may use at most 32 MiB of HBM per device.

v0:
```python
import jax
import jax.numpy as jnp
from jax import lax
from jax.sharding import PartitionSpec as P

time_step = 0.02
remap_table = ((0.45, 0.4, 0.15, 0.0), (0.0, 0.15, 0.4, 0.45))
gll_points = (-1.0, -0.4472135954999579, 0.4472135954999579, 1.0)


def extended(array, sides, width):
    for axis, dim in sides:
        count, length = (lax.axis_size(axis), array.shape[dim])
        up = [(i, (i + 1) % count) for i in range(count)]
        down = [(j, i) for i, j in up]
        last = lax.slice_in_dim(array, length - width, length, axis=dim)
        leading = lax.slice_in_dim(array, 0, width, axis=dim)
        before = lax.ppermute(last, axis, up)
        after = lax.ppermute(leading, axis, down)
        array = jnp.concatenate([before, array, after], axis=dim)
    return array


def gll_matrix():
    matrix = []
    for row_idx in range(4):
        entries = []
        for col_idx in range(4):
            if row_idx == col_idx:
                running = 0.0
                for third_idx in range(4):
                    if third_idx != row_idx:
                        running += 1.0 / (gll_points[row_idx] - gll_points[third_idx])
                entries.append(2.0 * running)
            else:
                numerator = 1.0
                denominator = 1.0
                for third_idx in range(4):
                    if third_idx != row_idx:
                        numerator *= gll_points[row_idx] - gll_points[third_idx]
                    if third_idx != col_idx:
                        denominator *= gll_points[col_idx] - gll_points[third_idx]
                entries.append(
                    2.0 * numerator / (denominator * (gll_points[row_idx] - gll_points[col_idx]))
                )
        matrix.append(entries)
    return matrix


def derivatives(values):
    derivative = jnp.array(gll_matrix(), jnp.float32)
    layout = values.shape
    blocks_x = values.reshape(layout[:-2] + (layout[-2] // 4, 4, layout[-1]))
    along_x = jnp.einsum(
        "ij,...ejy->...eiy", derivative, blocks_x, precision=lax.Precision.HIGHEST
    ).reshape(layout)
    blocks_y = values.reshape(layout[:-1] + (layout[-1] // 4, 4))
    along_y = jnp.einsum(
        "ij,...ej->...ei", derivative, blocks_y, precision=lax.Precision.HIGHEST
    ).reshape(layout)
    return (along_x, along_y)


def tendency(tracer_vals, wind_vals):
    along_x, along_y = derivatives(tracer_vals)
    speeds = wind_vals.astype(jnp.float32)
    return -(speeds[0] * along_x + speeds[1] * along_y)


def remap_columns(stacked):
    weights_table = jnp.array(remap_table, jnp.float32)
    layout = stacked.shape
    blocks = stacked.reshape(layout[:-2] + (layout[-2] // 4, 4, layout[-1] // 4, 4))
    cell_values = jnp.einsum(
        "pa,qb,...xayb->...xpyq",
        weights_table,
        weights_table,
        blocks,
        precision=lax.Precision.HIGHEST,
    )
    return cell_values.reshape(layout[:-2] + (layout[-2] // 2, layout[-1] // 2))


def network_step(column_state, weight_in, weight_out):
    hidden = jax.nn.gelu(
        jnp.dot(column_state.astype(jnp.bfloat16), weight_in, preferred_element_type=jnp.float32)
    ).astype(jnp.bfloat16)
    return column_state + jnp.dot(hidden, weight_out, preferred_element_type=jnp.float32)


def pass_first(values):
    channels, extent, across = values.shape
    elements = extent // 4
    blocks = values.reshape(channels, elements, 4, across)
    edge_rows = jnp.stack([blocks[:, :, 0], blocks[:, :, 3]], axis=2).reshape(
        channels, 2 * elements, across
    )
    padded = extended(edge_rows.astype(jnp.bfloat16), (("grp", 1),), 1).astype(edge_rows.dtype)
    paired = padded.reshape(channels, elements + 1, 2, across).sum(axis=2)
    rebuilt = jnp.concatenate(
        [paired[:, :-1, None], blocks[:, :, 1:3], paired[:, 1:, None]], axis=2
    )
    return rebuilt.reshape(channels, extent, across)


def pass_second(values):
    channels, extent, across = values.shape
    elements = across // 4
    blocks = values.reshape(channels, extent, elements, 4)
    edge_rows = jnp.stack([blocks[..., 0], blocks[..., 3]], axis=3).reshape(
        channels, extent, 2 * elements
    )
    padded = extended(edge_rows.astype(jnp.bfloat16), (("bal", 2),), 1).astype(edge_rows.dtype)
    paired = padded.reshape(channels, extent, elements + 1, 2).sum(axis=3)
    rebuilt = jnp.concatenate(
        [paired[..., :-1, None], blocks[..., 1:3], paired[..., 1:, None]], axis=3
    )
    return rebuilt.reshape(channels, extent, across)


def home_columns(columns, cost_flat, weight_in, weight_out):
    column_state = columns.astype(jnp.float32)
    for substep in range(3):
        stepped = network_step(column_state, weight_in, weight_out)
        column_state = jnp.where((cost_flat > substep)[:, None], stepped, column_state)
    return column_state.astype(jnp.bfloat16)


def shards(tracers, winds, node_mass, column_cost, weight_in, weight_out):
    levels = tracers.shape[1]
    extent, across = node_mass.shape
    weighted = tendency(tracers, winds) * node_mass
    channels = jnp.concatenate(
        [weighted.reshape(2 * levels, extent, across), node_mass[None]], axis=0
    )
    summed = pass_second(pass_first(channels))
    averaged = summed[:-1] / summed[-1:]
    tracers_next = tracers + time_step * averaged.reshape(tracers.shape)
    stacked = jnp.concatenate([tracers_next, winds.astype(jnp.float32)], axis=0)
    cell_values = remap_columns(stacked).astype(jnp.bfloat16)
    columns = cell_values.reshape(4 * levels, -1).T
    cost_flat = column_cost.reshape(-1)
    result = home_columns(columns, cost_flat, weight_in, weight_out)
    columns_out = result.T.reshape(cell_values.shape)
    return (tracers_next, columns_out)


def solution(mesh):
    placed = (
        P(None, None, "grp", "bal"),
        P(None, None, "grp", "bal"),
        P("grp", "bal"),
        P("grp", "bal"),
        P(),
        P(),
    )
    return jax.shard_map(
        shards,
        mesh=mesh,
        in_specs=placed,
        out_specs=(P(None, None, "grp", "bal"), P(None, None, "grp", "bal")),
        check_vma=False,
    )
```

profile of v0, /device:TPU:1, one launch (start us, length us, event | category | flops | bytes accessed | tf_op | source)
XLA Modules:
  0.0 73.1 jit_solution(5609702766791364375)
XLA Ops:
  0.6 0.0 copy-start
  0.6 0.0 copy-start.8
  0.7 0.8 %copy.57 = f32[1,4,256]{2,0,1:T(1,128)S(1)} copy(f32[1,4,256]{2,1,0:T(4,128)} %bitcast.132) | data formatting | bytes 8192 | tf_op jit(solution)/shard_map/broadcast_in_dim | solution.py:134
  1.4 1.4 %copy.53 = f32[2,64,4,256]{1,3,2,0:T(8,128)S(1)} copy(f32[2,64,4,256]{3,2,1,0:T(4,128)} %param.8) | data formatting | bytes 1048576 | tf_op args[0]
  2.8 0.8 %copy.54 = f32[2,64,4,64,4]{3,4,2,1,0:T(4,128)S(1)} copy(f32[2,64,4,64,4]{1,4,3,2,0:T(4,128)S(1)} %bitcast.120) | data formatting | bytes 1048576 | tf_op jit(solution)/shard_map/reshape | solution.py:57
  3.6 0.0 copy-done.8
  3.6 1.8 %convolution_bitcast_fusion = f32[2,64,4,64,4]{3,4,2,1,0:T(4,128)S(1)} fusion(f32[4,4,1,1,1]{1,0,4,3,2:T(4,128)S(1)} %copy-done.8, f32[2,64,4,64,4]{3,4,2,1,0:T(4,128)S(1)} %copy.54), kind=kOutput, calls=%fused_computation.4 | convolution fusion | flops 6291456 | bytes 1048640 | tf_op jit(solution)/shard_map/ij,...ej->...ei/dot_general | solution.py:58
  5.4 0.0 copy-start.1
  5.4 0.0 copy-start.7
  5.5 1.3 %copy.55 = f32[2,64,4,64,4]{1,0,4,3,2:T(2,128)} copy(f32[2,64,4,64,4]{3,4,2,1,0:T(4,128)S(1)} %convolution_bitcast_fusion) | data formatting | bytes 1048576 | tf_op jit(solution)/shard_map/ij,...ej->...ei/dot_general | solution.py:58
  6.8 1.9 %reshape.90 = f32[128,4,256]{0,2,1:T(8,128)S(1)} reshape(f32[2,64,4,64,4]{1,0,4,3,2:T(2,128)} %copy.55) | data formatting | bytes 1048576 | tf_op jit(solution)/shard_map/reshape | solution.py:60
  8.7 0.2 copy.56
  8.9 1.0 %fusion.83 = f32[4,2,64,256]{3,0,2,1:T(4,128)S(1)} fusion(f32[4,4,1,1]{1,0,3,2:T(4,128)S(1)} %copy-done.7, f32[2,64,4,256]{3,2,1,0:T(4,128)S(1)} %copy-done.1), kind=kOutput, calls=%fused_computation.96 | convolution fusion | flops 6291456 | bytes 1048640 | tf_op jit(solution)/shard_map/ij,...ejy->...eiy/dot_general | solution.py:54
  9.9 0.0 copy-start.5
  9.9 0.5 copy.49
  10.4 1.5 %fusion.76 = (f32[1,64,4,256]{1,0,3,2:T(1,128)S(1)}, f32[1,64,4,256]{1,0,3,2:T(1,128)}) fusion(bf16[2,64,4,256]{1,0,3,2:T(2,128)(2,1)S(1)} %copy.49), kind=kLoop, calls=%fused_computation.90 | loop fusion | bytes 1048576 | tf_op jit(solution)/shard_map/slice | solution.py:67
  11.9 1.2 %copy.52 = f32[64,4,256]{2,0,1:T(8,128)S(1)} copy(f32[64,4,256]{0,2,1:T(8,128)} %bitcast.127) | data formatting | bytes 524288 | tf_op jit(solution)/shard_map/mul | solution.py:67
  13.2 0.9 %copy.50 = f32[64,4,256]{2,0,1:T(8,128)} copy(f32[64,4,256]{0,2,1:T(8,128)S(1)} %bitcast.126) | data formatting | bytes 524288 | tf_op jit(solution)/shard_map/mul | solution.py:67
  14.0 0.0 copy-done.5
  14.0 1.1 %fusion.32 = f32[128,4,256]{2,0,1:T(8,128)S(1)} fusion(f32[128,4,256]{2,0,1:T(8,128)S(1)} %copy.56, f32[128,4,256]{2,1,0:T(4,128)S(1)} %bitcast.125, f32[4,256]{1,0:T(4,128)S(1)} %copy-done.5, f32[64,4,256]{2,0,1:T(8,128)S(1)} %copy.52, f32[64,4,256]{2,0,1:T(8,128)} %copy.50), kind=kLoop, calls=%fused_computation.46 | loop fusion | flops 655360 | bytes 2101248 | tf_op jit(solution)/shard_map/mul | solution.py:132
  15.2 0.0 copy-start.9
  15.3 0.6 fusion.80
  15.9 7.7 %collective-permute-start.1 = (bf16[129,1,256]{2,0,1:T(8,128)(2,1)}, bf16[129,1,256]{2,0,1:T(8,128)(2,1)S(1)}, u32[]{:S(2)}, u32[]{:S(2)}) collective-permute-start(bf16[129,1,256]{2,0,1:T(8,128)(2,1)} %get-tuple-element.23), channel_id=1, source_target_pairs={{64,0},{128,64},{192,128},{256,192},{320,256},{384,320},{448,384},... | collective-permute-start | bytes 198152 | tf_op jit(solution)/shard_map/ppermute | solution.py:19
  23.6 2.1 %collective-permute-start = (bf16[129,1,256]{2,0,1:T(8,128)(2,1)S(1)}, bf16[129,1,256]{2,0,1:T(8,128)(2,1)S(1)}, u32[]{:S(2)}, u32[]{:S(2)}) collective-permute-start(bf16[129,1,256]{2,0,1:T(8,128)(2,1)S(1)} %get-tuple-element.22), channel_id=1, source_target_pairs={{0,64},{64,128},{128,192},{192,256},{256,320},{320,384},{384,448},... | collective-permute-start | bytes 198152 | tf_op jit(solution)/shard_map/ppermute | solution.py:18
  25.7 0.7 copy.65
  26.3 1.3 %convert_element_type.68 = f32[2,64,4,256]{1,0,3,2:T(2,128)} convert(bf16[2,64,4,256]{1,0,3,2:T(2,128)(2,1)S(1)} %copy.49) | non-fusion elementwise | flops 131072 | bytes 786432 | tf_op jit(solution)/shard_map/convert_element_type | solution.py:66
  27.8 0.2 copy.59
  28.0 0.0 collective-permute-done.1
  28.0 3.9 %collective-permute-done = bf16[129,1,256]{2,0,1:T(8,128)(2,1)S(1)} collective-permute-done((bf16[129,1,256]{2,0,1:T(8,128)(2,1)S(1)}, bf16[129,1,256]{2,0,1:T(8,128)(2,1)S(1)}, u32[]{:S(2)}, u32[]{:S(2)}) %collective-permute-start) | collective-permute-done | bytes 66080 | tf_op jit(solution)/shard_map/ppermute | solution.py:18
  32.0 0.2 copy.60
  32.2 0.2 copy.58
  32.4 0.0 copy-start.3
  32.4 0.8 %fusion.74 = bf16[129,4,64,4]{0,1,3,2:T(4,128)(2,1)S(1)} fusion(f32[129,1,64,4]{0,1,3,2:T(1,128)S(1)} %bitcast.121, f32[129,2,64,4]{0,1,3,2:T(2,128)S(1)} %bitcast.118, f32[129,1,64,4]{0,1,3,2:T(1,128)S(1)} %bitcast.123), kind=kLoop, calls=%fused_computation.88 | loop fusion | flops 792576 | bytes 792576 | tf_op jit(solution)/shard_map/convert.6
  33.2 0.1 fusion.75
  33.3 0.2 pad_maximum_fusion.5
  33.5 9.6 %collective-permute-start.3 = (bf16[129,4,1]{0,1,2:T(4,128)(2,1)S(1)}, bf16[129,4,1]{0,1,2:T(4,128)(2,1)S(1)}, u32[]{:S(2)}, u32[]{:S(2)}) collective-permute-start(bf16[129,4,1]{0,1,2:T(4,128)(2,1)S(1)} %get-tuple-element.21), channel_id=1, source_target_pairs={{1,0},{2,1},{3,2},{4,3},{5,4},{6,5},{7,6},{8,7},{9,8},{10,9},{11,1... | collective-permute-start | bytes 3104 | tf_op jit(solution)/shard_map/ppermute | solution.py:19
  43.1 0.0 collective-permute-start.2
  43.1 1.7 %pad_maximum_fusion.1 = f32[129,4,64,4]{0,1,3,2:T(4,128)S(1)} fusion(f32[129,1,64,4]{0,1,3,2:T(1,128)S(1)} %bitcast.122, f32[129,2,64,4]{0,1,3,2:T(2,128)S(1)} %bitcast.119, f32[129,1,64,4]{0,1,3,2:T(1,128)} %bitcast.124), kind=kLoop, calls=%fused_computation.35 | loop fusion | flops 264192 | bytes 1056768 | tf_op jit(solution)/shard_map/concatenate | solution.py:100
  44.9 0.0 collective-permute-done.3
  44.9 6.2 %collective-permute-done.2 = bf16[129,4,1]{0,1,2:T(4,128)(2,1)S(1)} collective-permute-done((bf16[129,4,1]{0,1,2:T(4,128)(2,1)S(1)}, bf16[129,4,1]{0,1,2:T(4,128)(2,1)S(1)}, u32[]{:S(2)}, u32[]{:S(2)}) %collective-permute-start.2) | collective-permute-done | bytes 1064 | tf_op jit(solution)/shard_map/ppermute | solution.py:18
  51.1 0.2 pad_maximum_fusion.4
  51.3 0.2 convert_reduce_fusion.1
  51.4 0.1 slice_bitcast_fusion.1
  51.5 0.3 pad_maximum_fusion.2
  51.8 0.1 slice.97
  51.9 0.4 slice_reduce_fusion
  52.3 0.1 copy.63
  52.5 1.7 %slice.79 = f32[2,64,4,256]{1,0,3,2:T(2,128)} reshape(f32[128,4,64,4]{0,3,2,1:T(4,128)S(1)} %copy.63) | data formatting | bytes 1048576 | tf_op jit(solution)/shard_map/slice | solution.py:137
  54.2 0.1 copy.77
  54.2 2.9 %multiply_add_fusion = f32[2,64,4,256]{1,0,3,2:T(2,128)S(1)} fusion(f32[2,64,4,256]{1,0,3,2:T(2,128)S(1)} %copy.65, f32[2,64,4,256]{1,0,3,2:T(2,128)} %slice.79, f32[4,256]{1,0:T(4,128)S(1)} %copy.77), kind=kLoop, calls=%fused_computation.38 | loop fusion | flops 393216 | bytes 1576960 | tf_op jit(solution)/shard_map/add | solution.py:138
  57.2 1.2 %copy.71 = f32[2,64,4,256]{3,2,1,0:T(4,128)} copy(f32[2,64,4,256]{1,0,3,2:T(2,128)S(1)} %multiply_add_fusion) | data formatting | bytes 1048576
  58.4 0.1 copy-done.2
  58.4 2.5 %pad_maximum_fusion = f32[4,64,4,256]{1,0,3,2:T(4,128)} fusion(f32[2,64,4,256]{1,0,3,2:T(2,128)S(1)} %copy-done.2, f32[2,64,4,256]{1,0,3,2:T(2,128)S(1)} %multiply_add_fusion), kind=kLoop, calls=%fused_computation | loop fusion | flops 262144 | bytes 2097152 | tf_op jit(solution)/shard_map/concatenate | solution.py:139
  60.9 2.9 %copy.67 = f32[4,64,4,64,4]{3,2,4,1,0:T(4,128)S(1)} copy(f32[4,64,4,64,4]{1,0,4,3,2:T(4,128)} %bitcast.117) | data formatting | bytes 2097152 | tf_op jit(solution)/shard_map/reshape.4
  63.8 0.0 copy-start.10
  63.8 4.1 %fusion.84 = f32[4,64,64,4,2]{2,4,3,1,0:T(2,128)S(1)} fusion(f32[4,64,4,64,4]{3,2,4,1,0:T(4,128)S(1)} %copy.67, f32[2,4,1,1,1]{1,0,4,3,2:T(2,128)S(1)} %copy-done.6), kind=kOutput, calls=%fused_computation.97 | convolution fusion | flops 6291456 | bytes 1572896 | tf_op jit(solution)/shard_map/pa,qb,...xayb->...xpyq/dot_general | solution.py:74
  67.9 1.9 %fusion = bf16[4,64,1,2,64,2]{4,5,3,1,0,2:T(2,128)(2,1)S(1)} fusion(f32[2,4,1,1,1]{1,0,4,3,2:T(2,128)S(1)} %copy-done.6, f32[4,64,64,4,2]{2,4,3,1,0:T(2,128)S(1)} %fusion.84), kind=kOutput, calls=%fused_computation.6 | convolution fusion | flops 3211264 | bytes 655392 | tf_op jit(solution)/shard_map/pa,qb,...xayb->...xpyq/dot_general | solution.py:74
  69.8 0.2 copy.69
  70.1 0.2 convert_element_type.78
  70.3 0.6 fusion.39
  70.9 0.7 fusion.37
  71.6 0.7 fusion.3
  72.3 0.1 copy.70
  72.4 0.7 reshape.93
  (21 shorter events, 0.3 us)
Async XLA Ops:
  0.6 69.7 %copy-start = (bf16[1024,256]{1,0:T(8,128)(2,1)S(1)}, bf16[1024,256]{1,0:T(8,128)(2,1)}, u32[]{:S(2)}) copy-start(bf16[1024,256]{1,0:T(8,128)(2,1)} %param.13) | copy-start | bytes 1572868
  0.6 3.0 %copy-start.8 = (f32[4,4,1,1,1]{1,0,4,3,2:T(4,128)S(1)}, f32[4,4,1,1,1]{1,0,4,3,2:T(4,128)}, u32[]{:S(2)}) copy-start(f32[4,4,1,1,1]{1,0,4,3,2:T(4,128)} %constant.29) | copy-start | bytes 196
  5.4 3.4 %copy-start.1 = (f32[2,64,4,256]{3,2,1,0:T(4,128)S(1)}, f32[2,64,4,256]{3,2,1,0:T(4,128)}, u32[]{:S(2)}) copy-start(f32[2,64,4,256]{3,2,1,0:T(4,128)} %param.8) | copy-start | bytes 1572868
  5.4 3.4 %copy-start.7 = (f32[4,4,1,1]{1,0,3,2:T(4,128)S(1)}, f32[4,4,1,1]{1,0,3,2:T(4,128)}, u32[]{:S(2)}) copy-start(f32[4,4,1,1]{1,0,3,2:T(4,128)} %constant.28) | copy-start | bytes 196
  6.8 3.1 %copy-start.4 = (bf16[2,64,4,256]{3,2,1,0:T(4,128)(2,1)S(1)}, bf16[2,64,4,256]{3,2,1,0:T(4,128)(2,1)}, u32[]{:S(2)}) copy-start(bf16[2,64,4,256]{3,2,1,0:T(4,128)(2,1)} %param.9) | copy-start | bytes 786436
  9.9 4.2 %copy-start.5 = (f32[4,256]{1,0:T(4,128)S(1)}, f32[4,256]{1,0:T(4,128)}, u32[]{:S(2)}) copy-start(f32[4,256]{1,0:T(4,128)} %param.10) | copy-start | bytes 12292
  15.2 12.5 %copy-start.9 = (s32[2,128]{1,0:T(2,128)S(1)}, s32[2,128]{1,0:T(2,128)}, u32[]{:S(2)}) copy-start(s32[2,128]{1,0:T(2,128)} %param.11) | copy-start | bytes 3076
  15.9 12.1 %collective-permute-start.1 = (bf16[129,1,256]{2,0,1:T(8,128)(2,1)}, bf16[129,1,256]{2,0,1:T(8,128)(2,1)S(1)}, u32[]{:S(2)}, u32[]{:S(2)}) collective-permute-start(bf16[129,1,256]{2,0,1:T(8,128)(2,1)} %get-tuple-element.23), channel_id=1, source_target_pairs={{64,0},{128,64},{192,128},{256,192},{320,256},{384,320},{448,384},... | collective-permute-start | bytes 198152 | tf_op jit(solution)/shard_map/ppermute | solution.py:19
  23.6 8.4 %collective-permute-start = (bf16[129,1,256]{2,0,1:T(8,128)(2,1)S(1)}, bf16[129,1,256]{2,0,1:T(8,128)(2,1)S(1)}, u32[]{:S(2)}, u32[]{:S(2)}) collective-permute-start(bf16[129,1,256]{2,0,1:T(8,128)(2,1)S(1)} %get-tuple-element.22), channel_id=1, source_target_pairs={{0,64},{64,128},{128,192},{192,256},{256,320},{320,384},{384,448},... | collective-permute-start | bytes 198152 | tf_op jit(solution)/shard_map/ppermute | solution.py:18
  32.4 10.7 %copy-start.3 = (f32[129,1,256]{0,1,2:T(1,128)}, f32[129,1,256]{0,1,2:T(1,128)S(1)}, u32[]{:S(2)}) copy-start(f32[129,1,256]{0,1,2:T(1,128)S(1)} %copy.58) | copy-start | bytes 396292
  33.5 11.4 %collective-permute-start.3 = (bf16[129,4,1]{0,1,2:T(4,128)(2,1)S(1)}, bf16[129,4,1]{0,1,2:T(4,128)(2,1)S(1)}, u32[]{:S(2)}, u32[]{:S(2)}) collective-permute-start(bf16[129,4,1]{0,1,2:T(4,128)(2,1)S(1)} %get-tuple-element.21), channel_id=1, source_target_pairs={{1,0},{2,1},{3,2},{4,3},{5,4},{6,5},{7,6},{8,7},{9,8},{10,9},{11,1... | collective-permute-start | bytes 3104 | tf_op jit(solution)/shard_map/ppermute | solution.py:19
  43.1 8.0 %collective-permute-start.2 = (bf16[129,4,1]{0,1,2:T(4,128)(2,1)S(1)}, bf16[129,4,1]{0,1,2:T(4,128)(2,1)S(1)}, u32[]{:S(2)}, u32[]{:S(2)}) collective-permute-start(bf16[129,4,1]{0,1,2:T(4,128)(2,1)S(1)} %get-tuple-element.20), channel_id=1, source_target_pairs={{0,1},{1,2},{2,3},{3,4},{4,5},{5,6},{6,7},{7,8},{8,9},{9,10},{10,1... | collective-permute-start | bytes 3104 | tf_op jit(solution)/shard_map/ppermute | solution.py:18
  57.2 1.2 %copy-start.2 = (f32[2,64,4,256]{1,0,3,2:T(2,128)S(1)}, f32[2,64,4,256]{1,0,3,2:T(2,128)}, u32[]{:S(2)}) copy-start(f32[2,64,4,256]{1,0,3,2:T(2,128)} %convert_element_type.68) | copy-start | bytes 1572868
  60.9 2.9 %copy-start.6 = (f32[2,4,1,1,1]{1,0,4,3,2:T(2,128)S(1)}, f32[2,4,1,1,1]{1,0,4,3,2:T(2,128)}, u32[]{:S(2)}) copy-start(f32[2,4,1,1,1]{1,0,4,3,2:T(2,128)} %constant.30) | copy-start | bytes 100
  63.8 6.5 %copy-start.10 = (bf16[256,1024]{1,0:T(8,128)(2,1)S(1)}, bf16[256,1024]{1,0:T(8,128)(2,1)}, u32[]{:S(2)}) copy-start(bf16[256,1024]{1,0:T(8,128)(2,1)} %param.12) | copy-start | bytes 1572868
where the time goes:
time: 73.5 us; the launch traced here: 73.1 us
  local copies, waits for them, and re-layouts  20.4 us (28%)
  starting transfers between devices  19.3 us (26%)
  other arithmetic  11.4 us (16%)
  matrix products  10.7 us (15%)
  waiting for transfers between devices  10.1 us (14%)
  between operations  1.08 us (1%)
    ppermute x2, starting transfers between devices, extended(): after = lax.ppermute(leading, axis, down)  17.2 us
    ppermute x2, waiting for transfers between devices, extended(): before = lax.ppermute(last, axis, up)  10.1 us
    dot_general x2, matrix products, remap_columns(): jnp.einsum('pa,qb,...xayb->...xpyq', weights_table, weights_table, blocks...  6 us
    unnamed x26, local copies, waits for them, and re-layouts  3.83 us
    add x1, other arithmetic, shards(): tracers_next = tracers + time_step * averaged.reshape(tracers.shape)  2.91 us
    another operation x1, local copies, waits for them, and re-layouts  2.89 us
    concatenate x1, other arithmetic, shards(): stacked = jnp.concatenate([tracers_next, winds.astype(jnp.float32)], axis=0)  2.49 us
    slice x4, local copies, waits for them, and re-layouts, shards(): averaged = summed[:-1] / summed[-1:]  2.37 us
  transfers between devices with their start and end apart: 4, of which 2 were waited for; matrix products, arithmetic and copies ran while one was open for 6% of the time, Pallas kernels for 0%

commit v1 on v0

v1 whole, which is shorter than its diff:
```python
import functools

import jax
import jax.numpy as jnp
import ml_dtypes
import numpy as np
from jax import lax
from jax.experimental import pallas as pl
from jax.experimental.pallas import tpu as pltpu
from jax.sharding import PartitionSpec as P

time_step = 0.02
remap_table = ((0.45, 0.4, 0.15, 0.0), (0.0, 0.15, 0.4, 0.45))
gll_points = (-1.0, -0.4472135954999579, 0.4472135954999579, 1.0)
f32, bf16 = jnp.float32, jnp.bfloat16
CHUNK = 16
ROWS = 144
NT = (((1,), (1,)), ((), ()))


def gll_matrix():
    matrix = []
    for row_idx in range(4):
        entries = []
        for col_idx in range(4):
            if row_idx == col_idx:
                running = 0.0
                for third_idx in range(4):
                    if third_idx != row_idx:
                        running += 1.0 / (gll_points[row_idx] - gll_points[third_idx])
                entries.append(2.0 * running)
            else:
                numerator = 1.0
                denominator = 1.0
                for third_idx in range(4):
                    if third_idx != row_idx:
                        numerator *= gll_points[row_idx] - gll_points[third_idx]
                    if third_idx != col_idx:
                        denominator *= gll_points[col_idx] - gll_points[third_idx]
                entries.append(
                    2.0 * numerator / (denominator * (gll_points[row_idx] - gll_points[col_idx]))
                )
        matrix.append(entries)
    return matrix


def split_bf16(values):
    high = values.astype(np.float32).astype(ml_dtypes.bfloat16)
    low = (values.astype(np.float32) - high.astype(np.float32)).astype(ml_dtypes.bfloat16)
    return high, low


def lane_derivative():
    block = np.kron(np.eye(32), np.array(gll_matrix()).T)
    high, low = split_bf16(block)
    return np.block([[high, low], [high, np.zeros_like(low)]])


def lane_remap():
    high, low = split_bf16(np.kron(np.eye(64), np.array(remap_table)))
    return np.concatenate([high, low], axis=0)


def lane_index(shape):
    return lax.broadcasted_iota(jnp.int32, shape, 1)


def assemble_lanes(values):
    lane = lane_index(values.shape)
    inside = lane % 4
    first = jnp.logical_and(inside == 0, lane > 0)
    last = jnp.logical_and(inside == 3, lane < values.shape[1] - 1)
    return (
        values
        + jnp.where(first, pltpu.roll(values, 1, 1), 0.0)
        + jnp.where(last, pltpu.roll(values, values.shape[1] - 1, 1), 0.0)
    )


def edge_columns(planes):
    lane = lane_index((planes[0].shape[0], 128))
    left = jnp.zeros(lane.shape, f32)
    right = jnp.zeros(lane.shape, f32)
    for a in range(4):
        low, high = planes[a][:, :128], planes[a][:, 128:]
        left = jnp.where(lane == a, pltpu.roll(low, a, 1) if a else low, left)
        right = jnp.where(lane == 124 + a, pltpu.roll(high, 125 + a, 1) if a < 3 else high, right)
    return left, right


def tendency_kernel(t_ref, w_ref, m_ref, dy_ref, g_ref, gm_ref, up_ref, dn_ref, left_ref, right_ref, wf_ref):
    derivative = gll_matrix()
    mass = m_ref[...]
    wf_ref[...] = w_ref[...].astype(f32)
    mass_rows = assemble_lanes(jnp.concatenate([mass[0:4], mass[4:8]], axis=1))
    gm_ref[...] = mass_rows
    pad = jnp.zeros((ROWS - 129, 256), f32)
    up_ref[128:, :] = jnp.concatenate([mass_rows[3:4], pad], axis=0).astype(bf16)
    dn_ref[128:, :] = jnp.concatenate([mass_rows[0:1], pad], axis=0).astype(bf16)
    row_left, row_right = edge_columns([mass_rows[a : a + 1] for a in range(4)])
    pad = jnp.zeros((ROWS - 129, 128), f32)
    left_ref[128:, :] = jnp.concatenate([row_left, pad], axis=0)
    right_ref[128:, :] = jnp.concatenate([row_right, pad], axis=0)
    for k in range(2):
        for group in range(64 // CHUNK):
            level = group * CHUNK
            channel = k * 64 + level
            places = [(a, j) for a in range(4) for j in range(2)]
            x = {
                (a, j): t_ref[pl.ds(channel * 8 + j * 4 + a, CHUNK, stride=8), :]
                for a, j in places
            }
            lhs = []
            for place in places:
                high = x[place].astype(bf16)
                low = (x[place] - high.astype(f32)).astype(bf16)
                lhs.append(jnp.concatenate([high, low], axis=1))
            product = jnp.dot(
                jnp.concatenate(lhs, axis=0), dy_ref[...], preferred_element_type=f32
            )
            along_y = product[:, :128] + product[:, 128:]
            planes = []
            for a in range(4):
                halves = []
                for j in range(2):
                    along_x = derivative[a][0] * x[0, j]
                    for b in range(1, 4):
                        along_x += derivative[a][b] * x[b, j]
                    position = places.index((a, j)) * CHUNK
                    u = wf_ref[pl.ds(level * 8 + j * 4 + a, CHUNK, stride=8), :]
                    v = wf_ref[pl.ds(512 + level * 8 + j * 4 + a, CHUNK, stride=8), :]
                    total = u * along_x + v * along_y[position : position + CHUNK]
                    halves.append(-total * mass[j * 4 + a : j * 4 + a + 1, :])
                plane = assemble_lanes(jnp.concatenate(halves, axis=1))
                g_ref[a, channel : channel + CHUNK, :] = plane
                planes.append(plane)
            up_ref[channel : channel + CHUNK, :] = planes[3].astype(bf16)
            dn_ref[channel : channel + CHUNK, :] = planes[0].astype(bf16)
            left, right = edge_columns(planes)
            left_ref[channel : channel + CHUNK, :] = left
            right_ref[channel : channel + CHUNK, :] = right


def beside_kernel(w_ref, cost_ref, rt_ref, cells_ref, costs_ref, wf_ref, planes_ref):
    wf_ref[...] = w_ref[...].astype(f32)
    for k in range(2):
        for group in range(64 // CHUNK):
            channel = k * 64 + group * CHUNK
            sums = [None, None]
            for a in range(4):
                row = jnp.concatenate(
                    [
                        wf_ref[pl.ds(channel * 8 + j * 4 + a, CHUNK, stride=8), :]
                        for j in range(2)
                    ],
                    axis=1,
                )
                for p in range(2):
                    if remap_table[p][a]:
                        term = remap_table[p][a] * row
                        sums[p] = term if sums[p] is None else sums[p] + term
            for p in range(2):
                planes_ref[p, channel : channel + CHUNK, :] = sums[p].astype(bf16)
    eye = lax.broadcasted_iota(jnp.int32, (128, 128), 0) == lane_index((128, 128))
    for p in range(2):
        product = lax.dot_general(rt_ref[...], planes_ref[p], NT, preferred_element_type=f32)
        cells_ref[p * 128 : (p + 1) * 128, :] = (product[:128] + product[128:]).astype(bf16)
        diagonal = jnp.where(eye, cost_ref[p : p + 1, :].astype(f32), 0.0).astype(bf16)
        costs_ref[p * 128 : (p + 1) * 128, :] = jnp.dot(
            diagonal, jnp.ones((128, 128), bf16), preferred_element_type=f32
        )


def edges_kernel(left_ref, right_ref, r0_ref, r3_ref, to_left_ref, to_right_ref):
    lane = lane_index((ROWS, 128))
    r0 = r0_ref[...].astype(f32)
    r3 = r3_ref[...].astype(f32)
    left = left_ref[...] + jnp.where(lane == 0, r0[:, :128], 0.0)
    left += jnp.where(lane == 3, pltpu.roll(r3[:, :128], 3, 1), 0.0)
    right = right_ref[...] + jnp.where(lane == 127, r3[:, 128:], 0.0)
    right += jnp.where(lane == 124, pltpu.roll(r0[:, 128:], 125, 1), 0.0)
    to_left_ref[...] = left.astype(bf16)
    to_right_ref[...] = right.astype(bf16)


def gelu(x):
    inner = x * (0.7978845608028654 + 0.035677408136300125 * (x * x))
    half = 0.5 * x
    return half + half * jnp.tanh(inner)


def finish_kernel(
    t_ref, g_ref, gm_ref, r0_ref, r3_ref, cl_ref, cr_ref, cells_ref, costs_ref, rt_ref, wi_ref, wo_ref,
    t_out, c_out, planes_ref, turned_ref,
):
    def complete(a, own, start, size):
        if a == 0:
            own += r0_ref[start : start + 16, :].astype(f32)[:size]
        if a == 3:
            own += r3_ref[start : start + 16, :].astype(f32)[:size]
        lane = lane_index((size, 128))
        left = cl_ref[start : start + 16, :].astype(f32)[:size]
        right = cr_ref[start : start + 16, :].astype(f32)[:size]
        left = jnp.where(lane == 0, pltpu.roll(left, 4 - a, 1), 0.0)
        right = jnp.where(lane == 127, pltpu.roll(right, 127 - a, 1), 0.0)
        return jnp.concatenate([own[:, :128] + left, own[:, 128:] + right], axis=1)

    scale = [time_step / complete(a, gm_ref[a : a + 1, :], 128, 1) for a in range(4)]
    for channel in range(0, 128, CHUNK):
        sums = [None, None]
        for a in range(4):
            step = complete(a, g_ref[a, channel : channel + CHUNK, :], channel, CHUNK) * scale[a]
            halves = []
            for j in range(2):
                rows = pl.ds(channel * 8 + j * 4 + a, CHUNK, stride=8)
                value = t_ref[rows, :] + step[:, j * 128 : (j + 1) * 128]
                t_out[rows, :] = value
                halves.append(value)
            row = jnp.concatenate(halves, axis=1)
            for p in range(2):
                if remap_table[p][a]:
                    term = remap_table[p][a] * row
                    sums[p] = term if sums[p] is None else sums[p] + term
        for p in range(2):
            planes_ref[p, channel : channel + CHUNK, :] = sums[p].astype(bf16)
    states = []
    for p in range(2):
        product = lax.dot_general(rt_ref[...], planes_ref[p], NT, preferred_element_type=f32)
        tracer_cells = (product[:128] + product[128:]).astype(bf16).astype(f32)
        wind_cells = cells_ref[p * 128 : (p + 1) * 128, :].astype(f32)
        states.append(jnp.concatenate([tracer_cells, wind_cells], axis=1))
    state = jnp.concatenate(states, axis=0)
    costs = jnp.concatenate([costs_ref[...], costs_ref[...]], axis=1)
    for substep in range(3):
        rounded = state.astype(bf16)
        stepped = state
        for h in range(0, 1024, 256):
            hidden = jnp.dot(rounded, wi_ref[:, h : h + 256], preferred_element_type=f32)
            stepped += jnp.dot(
                gelu(hidden).astype(bf16), wo_ref[h : h + 256, :], preferred_element_type=f32
            )
        state = jnp.where(costs > substep, stepped, state)
    rounded = state.astype(bf16)
    eye = lax.broadcasted_iota(jnp.int32, (256, 256), 0) == lane_index((256, 256))
    eye = jnp.where(eye, 1.0, 0.0).astype(bf16)
    for p in range(2):
        turned_ref[pl.ds(p, 256, stride=2), :] = lax.dot_general(
            eye, rounded[p * 128 : (p + 1) * 128], NT, preferred_element_type=f32
        )
    c_out[...] = turned_ref[...].astype(bf16)


def call(kernel, outs, scratch, name):
    vmem = pl.BlockSpec(memory_space=pltpu.VMEM)
    shapes = tuple(jax.ShapeDtypeStruct(*o) for o in outs)

    def run(*args):
        return pl.pallas_call(
            kernel,
            out_shape=shapes,
            in_specs=[vmem] * len(args),
            out_specs=tuple(vmem for _ in outs),
            scratch_shapes=[pltpu.VMEM(*s) for s in scratch],
            compiler_params=pltpu.CompilerParams(vmem_limit_bytes=24 * 1024 * 1024),
            name=name,
        )(*args)

    return run


def node_rows(array):
    k, levels = array.shape[:2]
    return array.reshape(k, levels, 4, 2, 128).transpose(0, 1, 3, 2, 4).reshape(k * levels * 8, 128)


def shift(value, axis, by):
    count = lax.axis_size(axis)
    return lax.ppermute(value, axis, [(i, (i + by) % count) for i in range(count)])


def shards(tracers, winds, node_mass, column_cost, weight_in, weight_out):
    t = node_rows(tracers)
    w = node_rows(winds)
    m = node_mass.reshape(4, 2, 128).transpose(1, 0, 2).reshape(8, 128)
    g, gm, up, dn, left, right = call(
        tendency_kernel,
        [((4, 128, 256), f32), ((4, 256), f32), ((ROWS, 256), bf16), ((ROWS, 256), bf16), ((ROWS, 128), f32), ((ROWS, 128), f32)],
        [((1024, 128), f32)],
        "tendency",
    )(t, w, m, jnp.asarray(lane_derivative()))
    r0 = shift(up, "grp", 1)
    r3 = shift(dn, "grp", -1)
    remap = jnp.asarray(lane_remap())
    cells, costs = call(
        beside_kernel,
        [((256, 128), bf16), ((256, 128), f32)],
        [((1024, 128), f32), ((2, 128, 256), bf16)],
        "winds",
    )(w, column_cost, remap)
    to_left, to_right = call(
        edges_kernel, [((ROWS, 128), bf16), ((ROWS, 128), bf16)], [], "edges"
    )(left, right, r0, r3)
    cl = shift(to_right, "bal", 1)
    cr = shift(to_left, "bal", -1)
    t_next, columns = call(
        finish_kernel,
        [((1024, 128), f32), ((512, 128), bf16)],
        [((2, 128, 256), bf16), ((512, 128), f32)],
        "finish",
    )(t, g, gm, r0, r3, cl, cr, cells, costs, remap, weight_in, weight_out)
    t_next = t_next.reshape(2, 64, 2, 4, 128).transpose(0, 1, 3, 2, 4).reshape(2, 64, 4, 256)
    return t_next, columns.reshape(4, 64, 2, 128)


def solution(mesh):
    placed = (
        P(None, None, "grp", "bal"),
        P(None, None, "grp", "bal"),
        P("grp", "bal"),
        P("grp", "bal"),
        P(),
        P(),
    )
    return jax.shard_map(
        shards,
        mesh=mesh,
        in_specs=placed,
        out_specs=(P(None, None, "grp", "bal"), P(None, None, "grp", "bal")),
        check_vma=False,
    )
```

time: 73.5 us -> 38.4 us (0.52)
  the two profiles are of different devices: /device:TPU:1 before, /device:TPU:30 now
where the time goes in v1:
time: 38.4 us; the launch traced here: 38 us
  starting transfers between devices  19.7 us (51%)
  waiting for transfers between devices  8.93 us (23%)
  local copies, waits for them, and re-layouts  4.63 us (12%)
  Pallas kernels  4.05 us (11%)
  between operations  0.71 us (2%)
    ppermute x4, starting transfers between devices, shift(): lax.ppermute(value, axis, [(i, (i + by) % count) for i in range(count)])  19.7 us
    ppermute x4, waiting for transfers between devices, shift(): lax.ppermute(value, axis, [(i, (i + by) % count) for i in range(count)])  8.93 us
    unnamed x20, local copies, waits for them, and re-layouts  4.63 us
    pallas_call x4, Pallas kernels, run(): pl.pallas_call(kernel, out_shape=shapes, in_specs=[vmem] * len(args), out...  4.05 us
  transfers between devices with their start and end apart: 4, of which 2 were waited for; matrix products, arithmetic and copies ran while one was open for 0% of the time, Pallas kernels for 1%

profile of v1, /device:TPU:30, one launch (start us, length us, event | category | flops | bytes accessed | tf_op | source)
XLA Modules:
  0.0 38.0 jit_solution(13268467231594619959)
XLA Ops:
  0.6 0.0 copy-start.8
  0.6 0.7 %copy-done.8 = f32[4,256]{1,0:T(4,128)S(1)} copy-done((f32[4,256]{1,0:T(4,128)S(1)}, f32[4,256]{1,0:T(4,128)}, u32[]{:S(2)}) %copy-start.8) | copy-done | bytes 4120
  1.3 0.0 copy-start
  1.3 1.0 %copy-done = f32[2,64,4,256]{3,2,1,0:T(4,128)S(1)} copy-done((f32[2,64,4,256]{3,2,1,0:T(4,128)S(1)}, f32[2,64,4,256]{3,2,1,0:T(4,128)}, u32[]{:S(2)}) %copy-start) | copy-done | bytes 524312
  2.4 0.0 copy-start.2
  2.4 0.9 %copy-done.2 = bf16[2,64,4,256]{3,2,1,0:T(4,128)(2,1)S(1)} copy-done((bf16[2,64,4,256]{3,2,1,0:T(4,128)(2,1)S(1)}, bf16[2,64,4,256]{3,2,1,0:T(4,128)(2,1)}, u32[]{:S(2)}) %copy-start.2) | copy-done | bytes 262168
  3.3 0.0 copy-start.7
  3.3 0.9 %copy-done.7 = bf16[256,256]{1,0:T(8,128)(2,1)S(1)} copy-done((bf16[256,256]{1,0:T(8,128)(2,1)S(1)}, bf16[256,256]{1,0:T(8,128)(2,1)}, u32[]{:S(2)}) %copy-start.7) | copy-done | bytes 131096
  4.2 0.0 copy-start.3
  4.2 0.0 copy-start.6
  4.2 0.0 copy-start.9
  4.2 0.0 copy-start.4
  4.2 0.8 %tendency.1 = (f32[4,128,256]{2,1,0:T(8,128)S(1)}, f32[4,256]{1,0:T(4,128)S(1)}, bf16[144,256]{1,0:T(8,128)(2,1)S(1)}, bf16[144,256]{1,0:T(8,128)(2,1)S(1)}, f32...) custom-call(f32[1024,128]{1,0:T(8,128)S(1)} %bitcast.21, bf16[1024,128]{1,0:T(8,128)(2,1)S(1)} %bitcast.23, ...), custom_call_target="tpu_custom_call" | custom-call | tf_op jit(solution)/shard_map/tendency/pallas_call | solution.py:258
  5.0 0.0 copy-start.1
  5.0 14.8 %collective-permute-start = (bf16[144,256]{1,0:T(8,128)(2,1)S(1)}, bf16[144,256]{1,0:T(8,128)(2,1)S(1)}, u32[]{:S(2)}, u32[]{:S(2)}) collective-permute-start(bf16[144,256]{1,0:T(8,128)(2,1)S(1)} %get-tuple-element.16), channel_id=1, source_target_pairs={{0,64},{64,128},{128,192},{192,256},{256,320},{320,384},{384,448},... | collective-permute-start | bytes 221192 | tf_op jit(solution)/shard_map/ppermute | solution.py:278
  19.9 1.9 %collective-permute-start.1 = (bf16[144,256]{1,0:T(8,128)(2,1)S(1)}, bf16[144,256]{1,0:T(8,128)(2,1)S(1)}, u32[]{:S(2)}, u32[]{:S(2)}) collective-permute-start(bf16[144,256]{1,0:T(8,128)(2,1)S(1)} %get-tuple-element.17), channel_id=1, source_target_pairs={{0,960},{64,0},{128,64},{192,128},{256,192},{320,256},{384,320},{4... | collective-permute-start | bytes 221192 | tf_op jit(solution)/shard_map/ppermute | solution.py:278
  21.8 0.0 collective-permute-done.r0_ref
  21.8 7.6 %collective-permute-done.1.r3_ref = bf16[144,256]{1,0:T(8,128)(2,1)S(1)} collective-permute-done((bf16[144,256]{1,0:T(8,128)(2,1)S(1)}, bf16[144,256]{1,0:T(8,128)(2,1)S(1)}, u32[]{:S(2)}, u32[]{:S(2)}) %collective-permute-start.1) | collective-permute-done | bytes 73760 | tf_op jit(solution)/shard_map/ppermute | solution.py:278
  29.4 0.1 edges.1
  29.5 0.0 collective-permute-start.2
  29.6 2.9 %collective-permute-start.3 = (bf16[144,128]{1,0:T(8,128)(2,1)S(1)}, bf16[144,128]{1,0:T(8,128)(2,1)S(1)}, u32[]{:S(2)}, u32[]{:S(2)}) collective-permute-start(bf16[144,128]{1,0:T(8,128)(2,1)S(1)} %get-tuple-element.21), channel_id=1, source_target_pairs={{0,63},{1,0},{2,1},{3,2},{4,3},{5,4},{6,5},{7,6},{8,7},{9,8},{10,9... | collective-permute-start | bytes 110600 | tf_op jit(solution)/shard_map/ppermute | solution.py:278
  32.5 0.0 copy-done.3
  32.5 0.0 copy-done.6
  32.5 0.0 copy-done.9
  32.5 0.3 winds.1
  32.9 1.3 %collective-permute-done.2.cl_ref = bf16[144,128]{1,0:T(8,128)(2,1)S(1)} collective-permute-done((bf16[144,128]{1,0:T(8,128)(2,1)S(1)}, bf16[144,128]{1,0:T(8,128)(2,1)S(1)}, u32[]{:S(2)}, u32[]{:S(2)}) %collective-permute-start.2) | collective-permute-done | bytes 36896 | tf_op jit(solution)/shard_map/ppermute | solution.py:278
  34.1 0.0 collective-permute-done.3.cr_ref
  34.1 0.0 copy-done.4
  34.2 0.0 copy-done.1
  34.2 0.0 copy-start.5
  34.2 1.0 %copy-done.5 = bf16[1024,256]{1,0:T(8,128)(2,1)S(1)} copy-done((bf16[1024,256]{1,0:T(8,128)(2,1)S(1)}, bf16[1024,256]{1,0:T(8,128)(2,1)}, u32[]{:S(2)}) %copy-start.5) | copy-done | bytes 524312
  35.2 2.8 %finish.1 = (f32[1024,128]{1,0:T(8,128)}, bf16[512,128]{1,0:T(8,128)(2,1)}) custom-call(f32[1024,128]{1,0:T(8,128)S(1)} %bitcast.22, f32[4,128,256]{2,1,0:T(8,128)S(1)} %get-tuple-element.14.g_ref, f32[4,256]{1,0:T(4,128)S(1)} %get-tuple-element.15.gm_ref, bf16[144,256]{1,0:T(8,128)(2,1)S(1)} %collective-permute-done.r0_ref, ...), custom_call_target="tpu_custom_call" | custom-call | tf_op jit(solution)/shard_map/finish/pallas_call | solution.py:258
Async XLA Ops:
  0.6 0.7 %copy-start.8 = (f32[4,256]{1,0:T(4,128)S(1)}, f32[4,256]{1,0:T(4,128)}, u32[]{:S(2)}) copy-start(f32[4,256]{1,0:T(4,128)} %param.10) | copy-start | bytes 12292
  1.3 1.0 %copy-start = (f32[2,64,4,256]{3,2,1,0:T(4,128)S(1)}, f32[2,64,4,256]{3,2,1,0:T(4,128)}, u32[]{:S(2)}) copy-start(f32[2,64,4,256]{3,2,1,0:T(4,128)} %param.8) | copy-start | bytes 1572868
  2.4 0.9 %copy-start.2 = (bf16[2,64,4,256]{3,2,1,0:T(4,128)(2,1)S(1)}, bf16[2,64,4,256]{3,2,1,0:T(4,128)(2,1)}, u32[]{:S(2)}) copy-start(bf16[2,64,4,256]{3,2,1,0:T(4,128)(2,1)} %param.9) | copy-start | bytes 786436
  3.3 0.9 %copy-start.7 = (bf16[256,256]{1,0:T(8,128)(2,1)S(1)}, bf16[256,256]{1,0:T(8,128)(2,1)}, u32[]{:S(2)}) copy-start(bf16[256,256]{1,0:T(8,128)(2,1)} %constant.4.clone.dy_ref) | copy-start | bytes 393220
  4.2 28.3 %copy-start.3 = (bf16[2,64,4,256]{3,2,1,0:T(4,128)(2,1)S(1)}, bf16[2,64,4,256]{3,2,1,0:T(4,128)(2,1)}, u32[]{:S(2)}) copy-start(bf16[2,64,4,256]{3,2,1,0:T(4,128)(2,1)} %param.9) | copy-start | bytes 786436
  4.2 28.3 %copy-start.6 = (bf16[256,256]{1,0:T(8,128)(2,1)S(1)}, bf16[256,256]{1,0:T(8,128)(2,1)}, u32[]{:S(2)}) copy-start(bf16[256,256]{1,0:T(8,128)(2,1)} %constant.5.clone.rt_ref) | copy-start | bytes 393220
  4.2 28.3 %copy-start.9 = (s32[2,128]{1,0:T(2,128)S(1)}, s32[2,128]{1,0:T(2,128)}, u32[]{:S(2)}) copy-start(s32[2,128]{1,0:T(2,128)} %cost_ref.1) | copy-start | bytes 3076
  4.2 29.9 %copy-start.4 = (bf16[256,1024]{1,0:T(8,128)(2,1)S(1)}, bf16[256,1024]{1,0:T(8,128)(2,1)}, u32[]{:S(2)}) copy-start(bf16[256,1024]{1,0:T(8,128)(2,1)} %wi_ref.1) | copy-start | bytes 1572868
  5.0 29.1 %copy-start.1 = (f32[2,64,4,256]{3,2,1,0:T(4,128)S(1)}, f32[2,64,4,256]{3,2,1,0:T(4,128)}, u32[]{:S(2)}) copy-start(f32[2,64,4,256]{3,2,1,0:T(4,128)} %param.8) | copy-start | bytes 1572868
  5.0 16.8 %collective-permute-start = (bf16[144,256]{1,0:T(8,128)(2,1)S(1)}, bf16[144,256]{1,0:T(8,128)(2,1)S(1)}, u32[]{:S(2)}, u32[]{:S(2)}) collective-permute-start(bf16[144,256]{1,0:T(8,128)(2,1)S(1)} %get-tuple-element.16), channel_id=1, source_target_pairs={{0,64},{64,128},{128,192},{192,256},{256,320},{320,384},{384,448},... | collective-permute-start | bytes 221192 | tf_op jit(solution)/shard_map/ppermute | solution.py:278
  19.9 9.6 %collective-permute-start.1 = (bf16[144,256]{1,0:T(8,128)(2,1)S(1)}, bf16[144,256]{1,0:T(8,128)(2,1)S(1)}, u32[]{:S(2)}, u32[]{:S(2)}) collective-permute-start(bf16[144,256]{1,0:T(8,128)(2,1)S(1)} %get-tuple-element.17), channel_id=1, source_target_pairs={{0,960},{64,0},{128,64},{192,128},{256,192},{320,256},{384,320},{4... | collective-permute-start | bytes 221192 | tf_op jit(solution)/shard_map/ppermute | solution.py:278
  29.5 4.6 %collective-permute-start.2 = (bf16[144,128]{1,0:T(8,128)(2,1)S(1)}, bf16[144,128]{1,0:T(8,128)(2,1)S(1)}, u32[]{:S(2)}, u32[]{:S(2)}) collective-permute-start(bf16[144,128]{1,0:T(8,128)(2,1)S(1)} %get-tuple-element.20), channel_id=1, source_target_pairs={{0,1},{1,2},{2,3},{3,4},{4,5},{5,6},{6,7},{7,8},{8,9},{9,10},{10,1... | collective-permute-start | bytes 110600 | tf_op jit(solution)/shard_map/ppermute | solution.py:278
  29.6 4.6 %collective-permute-start.3 = (bf16[144,128]{1,0:T(8,128)(2,1)S(1)}, bf16[144,128]{1,0:T(8,128)(2,1)S(1)}, u32[]{:S(2)}, u32[]{:S(2)}) collective-permute-start(bf16[144,128]{1,0:T(8,128)(2,1)S(1)} %get-tuple-element.21), channel_id=1, source_target_pairs={{0,63},{1,0},{2,1},{3,2},{4,3},{5,4},{6,5},{7,6},{8,7},{9,8},{10,9... | collective-permute-start | bytes 110600 | tf_op jit(solution)/shard_map/ppermute | solution.py:278
  34.2 1.0 %copy-start.5 = (bf16[1024,256]{1,0:T(8,128)(2,1)S(1)}, bf16[1024,256]{1,0:T(8,128)(2,1)}, u32[]{:S(2)}) copy-start(bf16[1024,256]{1,0:T(8,128)(2,1)} %wo_ref.1) | copy-start | bytes 1572868

commit v2 on v1

v2 whole, which is shorter than its diff:
```python
import functools

import jax
import jax.numpy as jnp
import ml_dtypes
import numpy as np
from jax import lax
from jax.experimental import pallas as pl
from jax.experimental.pallas import tpu as pltpu
from jax.sharding import PartitionSpec as P

time_step = 0.02
remap_table = ((0.45, 0.4, 0.15, 0.0), (0.0, 0.15, 0.4, 0.45))
gll_points = (-1.0, -0.4472135954999579, 0.4472135954999579, 1.0)
f32, bf16 = jnp.float32, jnp.bfloat16
CHUNK = 16
ROWS = 144
NT = (((1,), (1,)), ((), ()))


def gll_matrix():
    matrix = []
    for row_idx in range(4):
        entries = []
        for col_idx in range(4):
            if row_idx == col_idx:
                running = 0.0
                for third_idx in range(4):
                    if third_idx != row_idx:
                        running += 1.0 / (gll_points[row_idx] - gll_points[third_idx])
                entries.append(2.0 * running)
            else:
                numerator = 1.0
                denominator = 1.0
                for third_idx in range(4):
                    if third_idx != row_idx:
                        numerator *= gll_points[row_idx] - gll_points[third_idx]
                    if third_idx != col_idx:
                        denominator *= gll_points[col_idx] - gll_points[third_idx]
                entries.append(
                    2.0 * numerator / (denominator * (gll_points[row_idx] - gll_points[col_idx]))
                )
        matrix.append(entries)
    return matrix


def split_bf16(values):
    high = values.astype(np.float32).astype(ml_dtypes.bfloat16)
    low = (values.astype(np.float32) - high.astype(np.float32)).astype(ml_dtypes.bfloat16)
    return high, low


def lane_derivative():
    block = np.kron(np.eye(32), np.array(gll_matrix()).T)
    high, low = split_bf16(block)
    return np.block([[high, low], [high, np.zeros_like(low)]])


def lane_remap():
    high, low = split_bf16(np.kron(np.eye(64), np.array(remap_table)))
    return np.concatenate([high, low], axis=0)


def lane_index(shape):
    return lax.broadcasted_iota(jnp.int32, shape, 1)


def assemble_lanes(values):
    lane = lane_index(values.shape)
    inside = lane % 4
    first = jnp.logical_and(inside == 0, lane > 0)
    last = jnp.logical_and(inside == 3, lane < values.shape[1] - 1)
    return (
        values
        + jnp.where(first, pltpu.roll(values, 1, 1), 0.0)
        + jnp.where(last, pltpu.roll(values, values.shape[1] - 1, 1), 0.0)
    )


def edge_columns(planes):
    lane = lane_index((planes[0].shape[0], 128))
    left = jnp.zeros(lane.shape, f32)
    right = jnp.zeros(lane.shape, f32)
    for a in range(4):
        low, high = planes[a][:, :128], planes[a][:, 128:]
        left = jnp.where(lane == a, pltpu.roll(low, a, 1) if a else low, left)
        right = jnp.where(lane == 124 + a, pltpu.roll(high, 125 + a, 1) if a < 3 else high, right)
    return left, right


def row_of(a):
    odd = lax.axis_index("grp") % 2
    return a + odd * (3 - 2 * a)


def weighted_rows(rows, channel, t_ref, wf_ref, mass, dy_ref):
    derivative = gll_matrix()
    sign = jnp.where(lax.axis_index("grp") % 2 == 1, -1.0, 1.0)
    level = channel % 64
    x = {
        (a, j): t_ref[pl.ds(channel * 8 + j * 4 + row_of(a), CHUNK, stride=8), :]
        for a in range(4)
        for j in range(2)
    }
    lhs = []
    for a in rows:
        for j in range(2):
            high = x[a, j].astype(bf16)
            low = (x[a, j] - high.astype(f32)).astype(bf16)
            lhs.append(jnp.concatenate([high, low], axis=1))
    product = jnp.dot(jnp.concatenate(lhs, axis=0), dy_ref[...], preferred_element_type=f32)
    along_y = product[:, :128] + product[:, 128:]
    planes = []
    for n, a in enumerate(rows):
        halves = []
        for j in range(2):
            along_x = derivative[a][0] * x[0, j]
            for b in range(1, 4):
                along_x += derivative[a][b] * x[b, j]
            position = (2 * n + j) * CHUNK
            u = wf_ref[pl.ds(level * 8 + j * 4 + row_of(a), CHUNK, stride=8), :]
            v = wf_ref[pl.ds(512 + level * 8 + j * 4 + row_of(a), CHUNK, stride=8), :]
            total = (sign * u) * along_x + v * along_y[position : position + CHUNK]
            halves.append(-total * mass[j * 4 + a : j * 4 + a + 1, :])
        planes.append(assemble_lanes(jnp.concatenate(halves, axis=1)))
    return planes


def tendency_kernel(
    t_hbm, w_hbm, m_hbm, dy_hbm, t_ref, wf_ref, mass_ref, dy_ref, g_ref, gm_ref, outer_ref, inner_ref,
    w_ref, m_ref, sems,
):
    copies = [
        pltpu.make_async_copy(source, target, sems.at[i])
        for i, (source, target) in enumerate(
            [(w_hbm, w_ref), (t_hbm, t_ref), (m_hbm, m_ref), (dy_hbm, dy_ref)]
        )
    ]
    for copy in copies:
        copy.start()
    for copy in copies:
        copy.wait()
    mass = m_ref[...]
    backward = jnp.concatenate([mass[i : i + 1] for i in (3, 2, 1, 0, 7, 6, 5, 4)], axis=0)
    mass = jnp.where(lax.axis_index("grp") % 2 == 1, backward, mass)
    mass_ref[...] = mass
    wf_ref[...] = w_ref[...].astype(f32)
    mass_rows = assemble_lanes(jnp.concatenate([mass[0:4], mass[4:8]], axis=1))
    gm_ref[...] = mass_rows
    pad = jnp.zeros((ROWS - 129, 256), f32)
    outer_ref[128:, :] = jnp.concatenate([mass_rows[0:1], pad], axis=0).astype(bf16)
    inner_ref[128:, :] = jnp.concatenate([mass_rows[3:4], pad], axis=0).astype(bf16)
    for channel in range(0, 128, CHUNK):
        rows = slice(channel, channel + CHUNK)
        planes = weighted_rows((0, 3), channel, t_ref, wf_ref, mass, dy_ref)
        for n, target in enumerate((outer_ref, inner_ref)):
            g_ref[n, rows, :] = planes[n]
            target[rows, :] = planes[n].astype(bf16)


def middle_kernel(t_ref, wf_ref, mass_ref, dy_ref, gm_ref, ends_ref, g_ref, left_ref, right_ref):
    mass = mass_ref[...]
    row_left, row_right = edge_columns([gm_ref[a : a + 1, :] for a in range(4)])
    pad = jnp.zeros((ROWS - 129, 128), f32)
    left_ref[128:, :] = jnp.concatenate([row_left, pad], axis=0)
    right_ref[128:, :] = jnp.concatenate([row_right, pad], axis=0)
    for channel in range(0, 128, CHUNK):
        rows = slice(channel, channel + CHUNK)
        planes = weighted_rows((1, 2), channel, t_ref, wf_ref, mass, dy_ref)
        for n in range(2):
            g_ref[n, rows, :] = planes[n]
        left, right = edge_columns([ends_ref[0, rows, :], *planes, ends_ref[1, rows, :]])
        left_ref[rows, :] = left
        right_ref[rows, :] = right


def beside_kernel(
    wf_ref, cost_ref, rt_ref, wi_hbm, wo_hbm, after_ref, cells_ref, costs_ref, wi_ref, wo_ref, planes_ref, sems
):
    first = pltpu.make_async_copy(wi_hbm, wi_ref, sems.at[0])
    second = pltpu.make_async_copy(wo_hbm, wo_ref, sems.at[1])
    first.start()
    second.start()
    for k in range(2):
        for group in range(64 // CHUNK):
            channel = k * 64 + group * CHUNK
            sums = [None, None]
            for a in range(4):
                row = jnp.concatenate(
                    [
                        wf_ref[pl.ds(channel * 8 + j * 4 + a, CHUNK, stride=8), :]
                        for j in range(2)
                    ],
                    axis=1,
                )
                for p in range(2):
                    if remap_table[p][a]:
                        term = remap_table[p][a] * row
                        sums[p] = term if sums[p] is None else sums[p] + term
            for p in range(2):
                planes_ref[p, channel : channel + CHUNK, :] = sums[p].astype(bf16)
    eye = lax.broadcasted_iota(jnp.int32, (128, 128), 0) == lane_index((128, 128))
    for p in range(2):
        product = lax.dot_general(rt_ref[...], planes_ref[p], NT, preferred_element_type=f32)
        cells_ref[p * 128 : (p + 1) * 128, :] = (product[:128] + product[128:]).astype(bf16)
        diagonal = jnp.where(eye, cost_ref[p : p + 1, :].astype(f32), 0.0).astype(bf16)
        costs_ref[p * 128 : (p + 1) * 128, :] = jnp.dot(
            diagonal, jnp.ones((128, 128), bf16), preferred_element_type=f32
        )
    first.wait()
    second.wait()


def with_columns(a, own, cl, cr):
    lane = lane_index(cl.shape)
    left = jnp.where(lane == 0, pltpu.roll(cl, 4 - a, 1), 0.0)
    right = jnp.where(lane == 127, pltpu.roll(cr, 127 - a, 1), 0.0)
    return jnp.concatenate([own[:, :128] + left, own[:, 128:] + right], axis=1)


def edges_kernel(left_ref, right_ref, r0_ref, r3_ref, to_left_ref, to_right_ref):
    lane = lane_index((ROWS, 128))
    r0 = r0_ref[...].astype(f32)
    r3 = r3_ref[...].astype(f32)
    left = left_ref[...] + jnp.where(lane == 0, r0[:, :128], 0.0)
    left += jnp.where(lane == 3, pltpu.roll(r3[:, :128], 3, 1), 0.0)
    right = right_ref[...] + jnp.where(lane == 127, r3[:, 128:], 0.0)
    right += jnp.where(lane == 124, pltpu.roll(r0[:, 128:], 125, 1), 0.0)
    to_left_ref[...] = left.astype(bf16)
    to_right_ref[...] = right.astype(bf16)


def gelu(x):
    inner = x * (0.7978845608028654 + 0.035677408136300125 * (x * x))
    half = 0.5 * x
    return half + half * jnp.tanh(inner)


def cell_row(p):
    odd = lax.axis_index("grp") % 2
    return p + odd * (1 - 2 * p)


def finish_kernel(
    t_ref, ends_ref, middle_ref, gm_ref, r0_ref, r3_ref, cl_ref, cr_ref, cells_ref, costs_ref, rt_ref, wi_ref, wo_ref,
    t_hbm, c_hbm, planes_ref, turned_ref, t_out, c_out, sems,
):
    def complete(a, own, start, size):
        rows = slice(start, start + CHUNK)
        if a in (0, 3):
            own += (r0_ref if a == 0 else r3_ref)[rows, :].astype(f32)[:size]
        return with_columns(a, own, cl_ref[rows, :].astype(f32)[:size], cr_ref[rows, :].astype(f32)[:size])

    scale = [time_step / complete(a, gm_ref[a : a + 1, :], 128, 1) for a in range(4)]
    for channel in range(0, 128, CHUNK):
        sums = [None, None]
        for a in range(4):
            source, n = (ends_ref, a // 3) if a in (0, 3) else (middle_ref, a - 1)
            change = complete(a, source[n, channel : channel + CHUNK, :], channel, CHUNK) * scale[a]
            halves = []
            for j in range(2):
                rows = pl.ds(channel * 8 + j * 4 + row_of(a), CHUNK, stride=8)
                value = t_ref[rows, :] + change[:, j * 128 : (j + 1) * 128]
                t_out[rows, :] = value
                halves.append(value)
            row = jnp.concatenate(halves, axis=1)
            for p in range(2):
                if remap_table[p][a]:
                    term = remap_table[p][a] * row
                    sums[p] = term if sums[p] is None else sums[p] + term
        for p in range(2):
            planes_ref[p, channel : channel + CHUNK, :] = sums[p].astype(bf16)
    store = pltpu.make_async_copy(t_out, t_hbm, sems.at[0])
    store.start()
    states, costs = [], []
    for p in range(2):
        product = lax.dot_general(rt_ref[...], planes_ref[p], NT, preferred_element_type=f32)
        tracer_cells = (product[:128] + product[128:]).astype(bf16).astype(f32)
        own = pl.ds(pl.multiple_of(cell_row(p) * 128, 128), 128)
        states.append(jnp.concatenate([tracer_cells, cells_ref[own, :].astype(f32)], axis=1))
        costs.append(jnp.concatenate([costs_ref[own, :], costs_ref[own, :]], axis=1))
    for substep in range(3):
        for p in range(2):
            rounded = states[p].astype(bf16)
            stepped = states[p]
            for h in range(0, 1024, 256):
                hidden = jnp.dot(rounded, wi_ref[:, h : h + 256], preferred_element_type=f32)
                stepped += jnp.dot(
                    gelu(hidden).astype(bf16), wo_ref[h : h + 256, :], preferred_element_type=f32
                )
            states[p] = jnp.where(costs[p] > substep, stepped, states[p])
    eye = lax.broadcasted_iota(jnp.int32, (256, 256), 0) == lane_index((256, 256))
    eye = jnp.where(eye, 1.0, 0.0).astype(bf16)
    for p in range(2):
        turned_ref[pl.ds(cell_row(p), 256, stride=2), :] = lax.dot_general(
            eye, states[p].astype(bf16), NT, preferred_element_type=f32
        )
    c_out[...] = turned_ref[...].astype(bf16)
    final = pltpu.make_async_copy(c_out, c_hbm, sems.at[1])
    final.start()
    store.wait()
    final.wait()


def call(kernel, outs, scratch, name, hbm_in=(), hbm_out=(), semaphores=0):
    shapes = tuple(jax.ShapeDtypeStruct(*o) for o in outs)
    scratch = [pltpu.VMEM(*s) for s in scratch]
    if semaphores:
        scratch.append(pltpu.SemaphoreType.DMA((semaphores,)))

    def spec(in_hbm):
        return pl.BlockSpec(memory_space=pltpu.HBM if in_hbm else pltpu.VMEM)

    def run(*args):
        args = [
            pltpu.with_memory_space_constraint(x, pltpu.HBM) if i in hbm_in else x
            for i, x in enumerate(args)
        ]
        return pl.pallas_call(
            kernel,
            out_shape=shapes,
            in_specs=[spec(i in hbm_in) for i in range(len(args))],
            out_specs=tuple(spec(i in hbm_out) for i in range(len(outs))),
            scratch_shapes=scratch,
            compiler_params=pltpu.CompilerParams(vmem_limit_bytes=24 * 1024 * 1024),
            name=name,
        )(*args)

    return run


def node_rows(array):
    k, levels = array.shape[:2]
    return array.reshape(k, levels, 4, 2, 128).transpose(0, 1, 3, 2, 4).reshape(k * levels * 8, 128)


def shift(value, axis, by):
    count = lax.axis_size(axis)
    return lax.ppermute(value, axis, [(i, (i + by) % count) for i in range(count)])


def shards(tracers, winds, node_mass, column_cost, weight_in, weight_out):
    t = node_rows(tracers)
    w = node_rows(winds)
    m = node_mass.reshape(4, 2, 128).transpose(1, 0, 2).reshape(8, 128)
    column, message = ((ROWS, 128), f32), ((ROWS, 256), bf16)
    pair, nodes = ((2, 128, 256), f32), ((1024, 128), f32)
    t, wf, mass, dy, ends, gm, outer, inner = call(
        tendency_kernel,
        [nodes, nodes, ((8, 128), f32), ((256, 256), bf16), pair, ((4, 256), f32), message, message],
        [((1024, 128), bf16), ((8, 128), f32)],
        "tendency",
        hbm_in=(0, 1, 2, 3),
        semaphores=4,
    )(t, w, m, jnp.asarray(lane_derivative()))
    middle, left, right = call(middle_kernel, [pair, column, column], [], "middle")(
        t, wf, mass, dy, gm, ends
    )
    count = lax.axis_size("grp")
    r0 = lax.ppermute(outer, "grp", [(i, (i + (1 if i % 2 else -1)) % count) for i in range(count)])
    r3 = lax.ppermute(inner, "grp", [(i, i ^ 1) for i in range(count)])
    column = ((ROWS, 128), bf16)
    to_left, to_right = call(edges_kernel, [column, column], [], "edges")(left, right, r0, r3)
    cl = shift(to_right, "bal", 1)
    cr = shift(to_left, "bal", -1)
    remap = jnp.asarray(lane_remap())
    cells, costs, first_weights, second_weights = call(
        beside_kernel,
        [((256, 128), bf16), ((256, 128), f32), ((256, 1024), bf16), ((1024, 256), bf16)],
        [((2, 128, 256), bf16)],
        "winds",
        hbm_in=(3, 4),
        semaphores=2,
    )(wf, column_cost, remap, weight_in, weight_out, to_left)
    t_next, columns = call(
        finish_kernel,
        [((1024, 128), f32), ((512, 128), bf16)],
        [((2, 128, 256), bf16), ((512, 128), f32), ((1024, 128), f32), ((512, 128), bf16)],
        "finish",
        hbm_out=(0, 1),
        semaphores=2,
    )(t, ends, middle, gm, r0, r3, cl, cr, cells, costs, remap, first_weights, second_weights)
    t_next = t_next.reshape(2, 64, 2, 4, 128).transpose(0, 1, 3, 2, 4).reshape(2, 64, 4, 256)
    return t_next, columns.reshape(4, 64, 2, 128)


def solution(mesh):
    placed = (
        P(None, None, "grp", "bal"),
        P(None, None, "grp", "bal"),
        P("grp", "bal"),
        P("grp", "bal"),
        P(),
        P(),
    )
    return jax.shard_map(
        shards,
        mesh=mesh,
        in_specs=placed,
        out_specs=(P(None, None, "grp", "bal"), P(None, None, "grp", "bal")),
        check_vma=False,
    )
```

time: 38.4 us -> 34 us (0.89)
  the two profiles are of different devices: /device:TPU:30 before, /device:TPU:2 now
where the time goes in v2:
time: 34 us; the launch traced here: 33.8 us
  starting transfers between devices  24.6 us (72%)
  Pallas kernels  6.33 us (19%)
  waiting for transfers between devices  2.11 us (6%)
  between operations  0.7 us (2%)
    ppermute x1, starting transfers between devices, shards(): r3 = lax.ppermute(inner, 'grp', [(i, i ^ 1) for i in range(count)])  13.6 us
    ppermute x2, starting transfers between devices, shift(): lax.ppermute(value, axis, [(i, (i + by) % count) for i in range(count)])  7.64 us
    pallas_call x5, Pallas kernels, run(): pl.pallas_call(kernel, out_shape=shapes, in_specs=[spec(i in hbm_in) for...  6.33 us
    ppermute x1, starting transfers between devices, shards(): lax.ppermute(outer, 'grp', [(i, (i + (1 if i % 2 else -1)) % count) for i...  3.4 us
    ppermute x1, waiting for transfers between devices, shards(): r3 = lax.ppermute(inner, 'grp', [(i, i ^ 1) for i in range(count)])  1.73 us
  transfers between devices with their start and end apart: 4, of which 2 were waited for; matrix products, arithmetic and copies ran while one was open for 0% of the time, Pallas kernels for 5%

profile of v2, /device:TPU:2, one launch (start us, length us, event | category | flops | bytes accessed | tf_op | source)
XLA Modules:
  0.0 33.8 jit_solution(17278426804526900236)
XLA Ops:
  0.6 1.7 %tendency.1 = (f32[1024,128]{1,0:T(8,128)S(1)}, f32[1024,128]{1,0:T(8,128)S(1)}, f32[8,128]{1,0:T(8,128)S(1)}, bf16[256,256]{1,0:T(8,128)(2,1)S(1)}, f32[2,128,2...) custom-call(f32[1024,128]{1,0:T(8,128)} %bitcast.21, ...), custom_call_target="tpu_custom_call" | custom-call | tf_op jit(solution)/shard_map/tendency/pallas_call | solution.py:319
  2.3 3.4 %collective-permute-start = (bf16[144,256]{1,0:T(8,128)(2,1)S(1)}, bf16[144,256]{1,0:T(8,128)(2,1)S(1)}, u32[]{:S(2)}, u32[]{:S(2)}) collective-permute-start(bf16[144,256]{1,0:T(8,128)(2,1)S(1)} %get-tuple-element.28), channel_id=1, source_target_pairs={{0,960},{64,128},{128,64},{192,256},{256,192},{320,384},{384,320},... | collective-permute-start | bytes 221192 | tf_op jit(solution)/shard_map/ppermute | solution.py:360
  5.8 13.6 %collective-permute-start.1 = (bf16[144,256]{1,0:T(8,128)(2,1)S(1)}, bf16[144,256]{1,0:T(8,128)(2,1)S(1)}, u32[]{:S(2)}, u32[]{:S(2)}) collective-permute-start(bf16[144,256]{1,0:T(8,128)(2,1)S(1)} %get-tuple-element.29), channel_id=1, source_target_pairs={{0,64},{64,0},{128,192},{192,128},{256,320},{320,256},{384,448},{4... | collective-permute-start | bytes 221192 | tf_op jit(solution)/shard_map/ppermute | solution.py:361
  19.4 0.6 %middle.1 = (f32[2,128,256]{2,1,0:T(8,128)S(1)}, f32[144,128]{1,0:T(8,128)S(1)}, f32[144,128]{1,0:T(8,128)S(1)}) custom-call(f32[1024,128]{1,0:T(8,128)S(1)} %get-tuple-element.21.t_ref, f32[1024,128]{1,0:T(8,128)S(1)} %get-tuple-element.23.wf_ref, f32[8,128]{1,0:T(8,128)S(1)} %get-tuple-element.24.mass_ref, bf16[256,256]{1,0:T(8,128)(2,1)S(1)} %get-tuple-element.25.dy_ref, ...), custom_call_target="tpu_custom_call" | custom-call | tf_op jit(solution)/shard_map/middle/pallas_call | solution.py:319
  19.9 0.0 collective-permute-done.r0_ref
  20.0 1.7 %collective-permute-done.1.r3_ref = bf16[144,256]{1,0:T(8,128)(2,1)S(1)} collective-permute-done((bf16[144,256]{1,0:T(8,128)(2,1)S(1)}, bf16[144,256]{1,0:T(8,128)(2,1)S(1)}, u32[]{:S(2)}, u32[]{:S(2)}) %collective-permute-start.1) | collective-permute-done | bytes 73760 | tf_op jit(solution)/shard_map/ppermute | solution.py:361
  21.7 0.0 copy-start
  21.7 0.1 edges.1
  21.8 0.0 copy-start.1
  21.8 0.0 collective-permute-start.2
  21.8 7.6 %collective-permute-start.3 = (bf16[144,128]{1,0:T(8,128)(2,1)S(1)}, bf16[144,128]{1,0:T(8,128)(2,1)S(1)}, u32[]{:S(2)}, u32[]{:S(2)}) collective-permute-start(bf16[144,128]{1,0:T(8,128)(2,1)S(1)} %get-tuple-element.33.after_ref), channel_id=1, source_target_pairs={{0,63},{1,0},{2,1},{3,2},{4,3},{5,4},{6,5},{7,6},{8,7},{9,8},{10,9... | collective-permute-start | bytes 110600 | tf_op jit(solution)/shard_map/ppermute | solution.py:339
  29.5 0.0 copy-done
  29.5 0.0 copy-done.1
  29.5 1.3 %winds.1 = (bf16[256,128]{1,0:T(8,128)(2,1)S(1)}, f32[256,128]{1,0:T(8,128)S(1)}, bf16[256,1024]{1,0:T(8,128)(2,1)S(1)}, bf16[1024,256]{1,0:T(8,128)(2,1)S(1)}) custom-call(f32[1024,128]{1,0:T(8,128)S(1)} %get-tuple-element.23.wf_ref, s32[2,128]{1,0:T(2,128)S(1)} %copy-done.1, bf16[256,256]{1,0:T(8,128)(2,1)S(1)} %copy-done, bf16[256,1024]{1,0:T(8,128)(2,1)} %wi_hbm.1, ...), custom_call_target="tpu_custom_call" | custom-call | tf_op jit(solution)/shard_map/winds/pallas_call | solution.py:319
  30.7 0.4 %collective-permute-done.2.cl_ref = bf16[144,128]{1,0:T(8,128)(2,1)S(1)} collective-permute-done((bf16[144,128]{1,0:T(8,128)(2,1)S(1)}, bf16[144,128]{1,0:T(8,128)(2,1)S(1)}, u32[]{:S(2)}, u32[]{:S(2)}) %collective-permute-start.2) | collective-permute-done | bytes 36896 | tf_op jit(solution)/shard_map/ppermute | solution.py:339
  31.1 0.0 collective-permute-done.3.cr_ref
  31.1 2.7 %finish.1 = (f32[1024,128]{1,0:T(8,128)}, bf16[512,128]{1,0:T(8,128)(2,1)}) custom-call(f32[1024,128]{1,0:T(8,128)S(1)} %get-tuple-element.21.t_ref, f32[2,128,256]{2,1,0:T(8,128)S(1)} %get-tuple-element.22.ends_ref, f32[2,128,256]{2,1,0:T(8,128)S(1)} %get-tuple-element.27.middle_ref, f32[4,256]{1,0:T(4,128)S(1)} %get-tuple-element.26.gm_ref, ...), custom_call_target="tpu_custom_call" | custom-call | tf_op jit(solution)/shard_map/finish/pallas_call | solution.py:319
Async XLA Ops:
  2.3 17.6 %collective-permute-start = (bf16[144,256]{1,0:T(8,128)(2,1)S(1)}, bf16[144,256]{1,0:T(8,128)(2,1)S(1)}, u32[]{:S(2)}, u32[]{:S(2)}) collective-permute-start(bf16[144,256]{1,0:T(8,128)(2,1)S(1)} %get-tuple-element.28), channel_id=1, source_target_pairs={{0,960},{64,128},{128,64},{192,256},{256,192},{320,384},{384,320},... | collective-permute-start | bytes 221192 | tf_op jit(solution)/shard_map/ppermute | solution.py:360
  5.8 15.9 %collective-permute-start.1 = (bf16[144,256]{1,0:T(8,128)(2,1)S(1)}, bf16[144,256]{1,0:T(8,128)(2,1)S(1)}, u32[]{:S(2)}, u32[]{:S(2)}) collective-permute-start(bf16[144,256]{1,0:T(8,128)(2,1)S(1)} %get-tuple-element.29), channel_id=1, source_target_pairs={{0,64},{64,0},{128,192},{192,128},{256,320},{320,256},{384,448},{4... | collective-permute-start | bytes 221192 | tf_op jit(solution)/shard_map/ppermute | solution.py:361
  21.7 7.8 %copy-start = (bf16[256,256]{1,0:T(8,128)(2,1)S(1)}, bf16[256,256]{1,0:T(8,128)(2,1)}, u32[]{:S(2)}) copy-start(bf16[256,256]{1,0:T(8,128)(2,1)} %constant.5.clone.rt_ref) | copy-start | bytes 393220
  21.8 7.7 %copy-start.1 = (s32[2,128]{1,0:T(2,128)S(1)}, s32[2,128]{1,0:T(2,128)}, u32[]{:S(2)}) copy-start(s32[2,128]{1,0:T(2,128)} %cost_ref.1) | copy-start | bytes 3076
  21.8 9.3 %collective-permute-start.2 = (bf16[144,128]{1,0:T(8,128)(2,1)S(1)}, bf16[144,128]{1,0:T(8,128)(2,1)S(1)}, u32[]{:S(2)}, u32[]{:S(2)}) collective-permute-start(bf16[144,128]{1,0:T(8,128)(2,1)S(1)} %get-tuple-element.32), channel_id=1, source_target_pairs={{0,1},{1,2},{2,3},{3,4},{4,5},{5,6},{6,7},{7,8},{8,9},{9,10},{10,1... | collective-permute-start | bytes 110600 | tf_op jit(solution)/shard_map/ppermute | solution.py:339
  21.8 9.3 %collective-permute-start.3 = (bf16[144,128]{1,0:T(8,128)(2,1)S(1)}, bf16[144,128]{1,0:T(8,128)(2,1)S(1)}, u32[]{:S(2)}, u32[]{:S(2)}) collective-permute-start(bf16[144,128]{1,0:T(8,128)(2,1)S(1)} %get-tuple-element.33.after_ref), channel_id=1, source_target_pairs={{0,63},{1,0},{2,1},{3,2},{4,3},{5,4},{6,5},{7,6},{8,7},{9,8},{10,9... | collective-permute-start | bytes 110600 | tf_op jit(solution)/shard_map/ppermute | solution.py:339

commit v3 on v2

--- a/solution.py
+++ b/solution.py
@@ -174,23 +174,14 @@
         right_ref[rows, :] = right
 
 
-def beside_kernel(
-    wf_ref, cost_ref, rt_ref, wi_hbm, wo_hbm, after_ref, cells_ref, costs_ref, wi_ref, wo_ref, planes_ref, sems
-):
-    first = pltpu.make_async_copy(wi_hbm, wi_ref, sems.at[0])
-    second = pltpu.make_async_copy(wo_hbm, wo_ref, sems.at[1])
-    first.start()
-    second.start()
+def wind_cells(wf_ref, cost_ref, rt_ref, cells_ref, costs_ref, planes_ref):
     for k in range(2):
         for group in range(64 // CHUNK):
             channel = k * 64 + group * CHUNK
             sums = [None, None]
             for a in range(4):
                 row = jnp.concatenate(
-                    [
-                        wf_ref[pl.ds(channel * 8 + j * 4 + a, CHUNK, stride=8), :]
-                        for j in range(2)
-                    ],
+                    [wf_ref[pl.ds(channel * 8 + j * 4 + a, CHUNK, stride=8), :] for j in range(2)],
                     axis=1,
                 )
                 for p in range(2):
@@ -207,6 +198,16 @@
         costs_ref[p * 128 : (p + 1) * 128, :] = jnp.dot(
             diagonal, jnp.ones((128, 128), bf16), preferred_element_type=f32
         )
+
+
+def beside_kernel(
+    wf_ref, cost_ref, rt_ref, wi_hbm, wo_hbm, after_ref, cells_ref, costs_ref, wi_ref, wo_ref, planes_ref, sems
+):
+    first = pltpu.make_async_copy(wi_hbm, wi_ref, sems.at[0])
+    second = pltpu.make_async_copy(wo_hbm, wo_ref, sems.at[1])
+    first.start()
+    second.start()
+    wind_cells(wf_ref, cost_ref, rt_ref, cells_ref, costs_ref, planes_ref)
     first.wait()
     second.wait()
 
@@ -241,46 +242,61 @@
     return p + odd * (1 - 2 * p)
 
 
-def finish_kernel(
-    t_ref, ends_ref, middle_ref, gm_ref, r0_ref, r3_ref, cl_ref, cr_ref, cells_ref, costs_ref, rt_ref, wi_ref, wo_ref,
-    t_hbm, c_hbm, planes_ref, turned_ref, t_out, c_out, sems,
-):
+def works_early():
+    me, last = lax.axis_index("grp"), lax.axis_size("grp") - 1
+    return jnp.logical_and(lax.axis_index("bal") == 0, jnp.logical_and(me != 0, me != last))
+
+
+def move_tracers(t_ref, ends_ref, middle_ref, gm_ref, r0_ref, r3_ref, columns, t_out, planes_ref, edges=None):
     def complete(a, own, start, size):
         rows = slice(start, start + CHUNK)
         if a in (0, 3):
             own += (r0_ref if a == 0 else r3_ref)[rows, :].astype(f32)[:size]
-        return with_columns(a, own, cl_ref[rows, :].astype(f32)[:size], cr_ref[rows, :].astype(f32)[:size])
+        if columns is None:
+            return own
+        return with_columns(a, own, *(ref[rows, :].astype(f32)[:size] for ref in columns))
 
     scale = [time_step / complete(a, gm_ref[a : a + 1, :], 128, 1) for a in range(4)]
     for channel in range(0, 128, CHUNK):
+        here = slice(channel, channel + CHUNK)
         sums = [None, None]
+        before, after = [], []
         for a in range(4):
             source, n = (ends_ref, a // 3) if a in (0, 3) else (middle_ref, a - 1)
-            change = complete(a, source[n, channel : channel + CHUNK, :], channel, CHUNK) * scale[a]
-            halves = []
+            change = complete(a, source[n, here, :], channel, CHUNK) * scale[a]
+            old, new = [], []
             for j in range(2):
                 rows = pl.ds(channel * 8 + j * 4 + row_of(a), CHUNK, stride=8)
-                value = t_ref[rows, :] + change[:, j * 128 : (j + 1) * 128]
-                t_out[rows, :] = value
-                halves.append(value)
-            row = jnp.concatenate(halves, axis=1)
+                old.append(t_ref[rows, :])
+                new.append(old[j] + change[:, j * 128 : (j + 1) * 128])
+                t_out[rows, :] = new[j]
+            row = jnp.concatenate(new, axis=1)
+            before.append(jnp.concatenate(old, axis=1))
+            after.append(row)
             for p in range(2):
                 if remap_table[p][a]:
                     term = remap_table[p][a] * row
                     sums[p] = term if sums[p] is None else sums[p] + term
         for p in range(2):
-            planes_ref[p, channel : channel + CHUNK, :] = sums[p].astype(bf16)
-    store = pltpu.make_async_copy(t_out, t_hbm, sems.at[0])
-    store.start()
-    states, costs = [], []
-    for p in range(2):
-        product = lax.dot_general(rt_ref[...], planes_ref[p], NT, preferred_element_type=f32)
-        tracer_cells = (product[:128] + product[128:]).astype(bf16).astype(f32)
-        own = pl.ds(pl.multiple_of(cell_row(p) * 128, 128), 128)
-        states.append(jnp.concatenate([tracer_cells, cells_ref[own, :].astype(f32)], axis=1))
-        costs.append(jnp.concatenate([costs_ref[own, :], costs_ref[own, :]], axis=1))
+            planes_ref[p, here, :] = sums[p].astype(bf16)
+        if edges is not None:
+            for target, values in zip(edges, (*edge_columns(before), *edge_columns(after))):
+                target[here, :] = values
+
+
+def own_cells(p):
+    return pl.ds(pl.multiple_of(cell_row(p) * 128, 128), 128)
+
+
+def entries(p, cells_ref, rt_ref, planes_ref):
+    product = lax.dot_general(rt_ref[...], planes_ref[p], NT, preferred_element_type=f32)
+    return jnp.concatenate([product[:128] + product[128:], cells_ref[own_cells(p), :].astype(f32)], axis=1)
+
+
+def network(states, costs, wi_ref, wo_ref):
+    states = [state.astype(bf16).astype(f32) for state in states]
     for substep in range(3):
-        for p in range(2):
+        for p in range(len(states)):
             rounded = states[p].astype(bf16)
             stepped = states[p]
             for h in range(0, 1024, 256):
@@ -289,12 +305,119 @@
                     gelu(hidden).astype(bf16), wo_ref[h : h + 256, :], preferred_element_type=f32
                 )
             states[p] = jnp.where(costs[p] > substep, stepped, states[p])
+    return states
+
+
+def turn(values):
     eye = lax.broadcasted_iota(jnp.int32, (256, 256), 0) == lane_index((256, 256))
-    eye = jnp.where(eye, 1.0, 0.0).astype(bf16)
+    return lax.dot_general(
+        jnp.where(eye, 1.0, 0.0).astype(bf16), values.astype(bf16), NT, preferred_element_type=f32
+    )
+
+
+def all_columns(states, costs_ref, wi_ref, wo_ref, turned_ref):
+    costs = [jnp.concatenate([costs_ref[own_cells(p), :]] * 2, axis=1) for p in range(2)]
+    for p, state in enumerate(network(states, costs, wi_ref, wo_ref)):
+        turned_ref[pl.ds(cell_row(p), 256, stride=2), :] = turn(state)
+
+
+def early_kernel(
+    t_ref, ends_ref, middle_ref, gm_ref, r0_ref, r3_ref, wf_ref, cost_hbm, rt_hbm, wi_hbm, wo_hbm,
+    t_out, x0_ref, turned_ref, *rest,
+):
+    *edges, planes_ref, wind_planes_ref, cells_ref, costs_ref, cost_ref, rt_ref, wi_ref, wo_ref, sems = rest
+
+    @pl.when(works_early())
+    def _():
+        sources, targets = (cost_hbm, rt_hbm, wi_hbm, wo_hbm), (cost_ref, rt_ref, wi_ref, wo_ref)
+        copies = [pltpu.make_async_copy(*pair, sems.at[i]) for i, pair in enumerate(zip(sources, targets))]
+        for copy in copies:
+            copy.start()
+        for copy in copies:
+            copy.wait()
+        wind_cells(wf_ref, cost_ref, rt_ref, cells_ref, costs_ref, wind_planes_ref)
+        move_tracers(t_ref, ends_ref, middle_ref, gm_ref, r0_ref, r3_ref, None, t_out, planes_ref, edges)
+        states = [entries(p, cells_ref, rt_ref, planes_ref) for p in range(2)]
+        for p in range(2):
+            x0_ref[p] = states[p]
+        all_columns(states, costs_ref, wi_ref, wo_ref, turned_ref)
+
+
+def correct(
+    early, to_left_ref, to_right_ref, cl_ref, cr_ref, costs_ref, wi_ref, wo_ref, t_out, turned_ref, store
+):
+    te_ref, x0_ref, before_turned_ref, *edges = early
+    lane = lane_index((128, 128))
+    changes = []
+    for side, (own_ref, other_ref) in enumerate(((to_left_ref, cl_ref), (to_right_ref, cr_ref))):
+        total = own_ref[...].astype(f32) + pltpu.roll(other_ref[...].astype(f32), 124 if side else 4, 1)
+        ours = lane_index((1, 128)) >= 124 if side else lane_index((1, 128)) < 4
+        scale = jnp.where(ours, time_step / jnp.where(ours, total[128:129], 1.0), 0.0)
+        new = edges[side][...] + total[:128] * scale
+        delta = jnp.where(ours, new - edges[2 + side][...], 0.0).astype(bf16)
+        weights = jnp.zeros((8, 128), f32)
+        row = lax.broadcasted_iota(jnp.int32, (8, 128), 0)
+        for p in range(2):
+            for a in range(4):
+                place = jnp.logical_and(row == p, lane_index((8, 128)) == (124 + a if side else a))
+                weights = jnp.where(place, remap_table[p][a] * remap_table[0][0], weights)
+        high = weights.astype(bf16)
+        low = (weights - high.astype(f32)).astype(bf16)
+        changes.append(
+            lax.dot_general(high, delta, NT, preferred_element_type=f32)
+            + lax.dot_general(low, delta, NT, preferred_element_type=f32)
+        )
+        for a in range(4):
+            rows = pl.ds(side * 4 + row_of(a), 128, stride=8)
+            moved = pltpu.roll(new, 3 - a if side else (128 - a) % 128, 1)
+            t_out[rows, :] = jnp.where(lane == (127 if side else 0), moved, te_ref[rows, :])
+    store.start()
+    row = lax.broadcasted_iota(jnp.int32, (8, 256), 0)
+    states, costs = [], []
     for p in range(2):
-        turned_ref[pl.ds(cell_row(p), 256, stride=2), :] = lax.dot_general(
-            eye, states[p].astype(bf16), NT, preferred_element_type=f32
+        ends = []
+        for side in range(2):
+            change = jnp.concatenate([changes[side][p : p + 1], jnp.zeros((1, 128), f32)], axis=1)
+            ends.append(x0_ref[p, side * 120 : side * 120 + 8, :] + change)
+        states.append(jnp.where(row == 0, ends[0], ends[1]))
+        first = pl.multiple_of(cell_row(p) * 128, 128)
+        ends = [jnp.concatenate([costs_ref[pl.ds(first + side * 120, 8), :]] * 2, axis=1) for side in range(2)]
+        costs.append(jnp.where(row == 0, ends[0], ends[1]))
+    (state,) = network(
+        [jnp.concatenate(states, axis=0)], [jnp.concatenate(costs, axis=0)], wi_ref, wo_ref
+    )
+    for p in range(2):
+        part = state[p * 8 : (p + 1) * 8]
+        top, bottom = jnp.where(row == 0, part, 0.0), jnp.where(row == 7, part, 0.0)
+        placed = turn(jnp.concatenate([top, jnp.zeros((112, 256), f32), bottom], axis=0))
+        rows = pl.ds(cell_row(p), 256, stride=2)
+        column = lane_index((256, 128))
+        changed = jnp.logical_or(column == 0, column == 127)
+        turned_ref[rows, :] = jnp.where(changed, placed, before_turned_ref[rows, :])
+
+
+def finish_kernel(
+    t_ref, ends_ref, middle_ref, gm_ref, r0_ref, r3_ref, cl_ref, cr_ref, to_left_ref, to_right_ref, cells_ref,
+    costs_ref, rt_ref, wi_ref, wo_ref, *rest,
+):
+    *early, t_hbm, c_hbm, planes_ref, turned_ref, t_out, c_out, sems = rest
+    store = pltpu.make_async_copy(t_out, t_hbm, sems.at[0])
+    ahead = works_early()
+
+    @pl.when(ahead)
+    def _():
+        correct(
+            early, to_left_ref, to_right_ref, cl_ref, cr_ref, costs_ref, wi_ref, wo_ref, t_out, turned_ref, store
         )
+
+    @pl.when(jnp.logical_not(ahead))
+    def _():
+        columns = (cl_ref, cr_ref)
+        move_tracers(t_ref, ends_ref, middle_ref, gm_ref, r0_ref, r3_ref, columns, t_out, planes_ref)
+        store.start()
+        states = [entries(p, cells_ref, rt_ref, planes_ref) for p in range(2)]
+        all_columns(states, costs_ref, wi_ref, wo_ref, turned_ref)
+
     c_out[...] = turned_ref[...].astype(bf16)
     final = pltpu.make_async_copy(c_out, c_hbm, sems.at[1])
     final.start()
@@ -361,12 +484,23 @@
     r3 = lax.ppermute(inner, "grp", [(i, i ^ 1) for i in range(count)])
     column = ((ROWS, 128), bf16)
     to_left, to_right = call(edges_kernel, [column, column], [], "edges")(left, right, r0, r3)
+    remap = jnp.asarray(lane_remap())
+    cells, costs, small = ((256, 128), bf16), ((256, 128), f32), ((128, 128), f32)
+    weights = [((256, 1024), bf16), ((1024, 256), bf16)]
+    early = call(
+        early_kernel,
+        [nodes, ((2, 128, 256), f32), ((512, 128), f32), small, small, small, small],
+        [((2, 128, 256), bf16), ((2, 128, 256), bf16), cells, costs, ((2, 128), jnp.int32), ((256, 256), bf16), *weights],
+        "early",
+        hbm_in=(7, 8, 9, 10),
+        semaphores=4,
+    )(t, ends, middle, gm, r0, r3, wf, column_cost, remap, weight_in, weight_out)
+    to_left, to_right, *early = lax.optimization_barrier((to_left, to_right, *early))
     cl = shift(to_right, "bal", 1)
     cr = shift(to_left, "bal", -1)
-    remap = jnp.asarray(lane_remap())
     cells, costs, first_weights, second_weights = call(
         beside_kernel,
-        [((256, 128), bf16), ((256, 128), f32), ((256, 1024), bf16), ((1024, 256), bf16)],
+        [cells, costs, *weights],
         [((2, 128, 256), bf16)],
         "winds",
         hbm_in=(3, 4),
@@ -379,7 +513,10 @@
         "finish",
         hbm_out=(0, 1),
         semaphores=2,
-    )(t, ends, middle, gm, r0, r3, cl, cr, cells, costs, remap, first_weights, second_weights)
+    )(
+        t, ends, middle, gm, r0, r3, cl, cr, to_left, to_right, cells, costs, remap, first_weights,
+        second_weights, *early,
+    )
     t_next = t_next.reshape(2, 64, 2, 4, 128).transpose(0, 1, 3, 2, 4).reshape(2, 64, 4, 256)
     return t_next, columns.reshape(4, 64, 2, 128)
 

time: 34 us -> 33.6 us (0.988)
  starting transfers between devices: 24.6 us -> 21.3 us
  Pallas kernels: 6.33 us -> 9.23 us
    ppermute x2, starting transfers between devices: 7.64 us -> 4.33 us  [shift(): lax.ppermute(value, axis, [(i, (i + by) % count) for i in range(count)])]
    pallas_call x5 -> x6, Pallas kernels: 6.33 us -> 9.23 us  [run(): pl.pallas_call(kernel, out_shape=shapes, in_specs=[spec(i in hbm_in) for...]
where the time goes in v3:
time: 33.6 us; the launch traced here: 33.4 us
  starting transfers between devices  21.3 us (63%)
  Pallas kernels  9.23 us (27%)
  waiting for transfers between devices  2.11 us (6%)
  between operations  0.72 us (2%)
    ppermute x1, starting transfers between devices, shards(): r3 = lax.ppermute(inner, 'grp', [(i, i ^ 1) for i in range(count)])  13.6 us
    pallas_call x6, Pallas kernels, run(): pl.pallas_call(kernel, out_shape=shapes, in_specs=[spec(i in hbm_in) for...  9.23 us
    ppermute x2, starting transfers between devices, shift(): lax.ppermute(value, axis, [(i, (i + by) % count) for i in range(count)])  4.33 us
    ppermute x1, starting transfers between devices, shards(): lax.ppermute(outer, 'grp', [(i, (i + (1 if i % 2 else -1)) % count) for i...  3.4 us
    ppermute x1, waiting for transfers between devices, shards(): r3 = lax.ppermute(inner, 'grp', [(i, i ^ 1) for i in range(count)])  1.74 us
  transfers between devices with their start and end apart: 4, of which 2 were waited for; matrix products, arithmetic and copies ran while one was open for 0% of the time, Pallas kernels for 5%

profile of v3, /device:TPU:2, one launch (start us, length us, event | category | flops | bytes accessed | tf_op | source)
XLA Modules:
  0.0 33.4 jit_solution(18308125858647745676)
XLA Ops:
  0.6 1.7 %tendency.1 = (f32[1024,128]{1,0:T(8,128)S(1)}, f32[1024,128]{1,0:T(8,128)S(1)}, f32[8,128]{1,0:T(8,128)S(1)}, bf16[256,256]{1,0:T(8,128)(2,1)S(1)}, f32[2,128,2...) custom-call(f32[1024,128]{1,0:T(8,128)} %bitcast.21, ...), custom_call_target="tpu_custom_call" | custom-call | tf_op jit(solution)/shard_map/tendency/pallas_call | solution.py:442
  2.3 3.4 %collective-permute-start = (bf16[144,256]{1,0:T(8,128)(2,1)S(1)}, bf16[144,256]{1,0:T(8,128)(2,1)S(1)}, u32[]{:S(2)}, u32[]{:S(2)}) collective-permute-start(bf16[144,256]{1,0:T(8,128)(2,1)S(1)} %get-tuple-element.44), channel_id=1, source_target_pairs={{0,960},{64,128},{128,64},{192,256},{256,192},{320,384},{384,320},... | collective-permute-start | bytes 221192 | tf_op jit(solution)/shard_map/ppermute | solution.py:483
  5.7 13.6 %collective-permute-start.1 = (bf16[144,256]{1,0:T(8,128)(2,1)S(1)}, bf16[144,256]{1,0:T(8,128)(2,1)S(1)}, u32[]{:S(2)}, u32[]{:S(2)}) collective-permute-start(bf16[144,256]{1,0:T(8,128)(2,1)S(1)} %get-tuple-element.45), channel_id=1, source_target_pairs={{0,64},{64,0},{128,192},{192,128},{256,320},{320,256},{384,448},{4... | collective-permute-start | bytes 221192 | tf_op jit(solution)/shard_map/ppermute | solution.py:484
  19.4 0.6 %middle.1 = (f32[2,128,256]{2,1,0:T(8,128)S(1)}, f32[144,128]{1,0:T(8,128)S(1)}, f32[144,128]{1,0:T(8,128)S(1)}) custom-call(f32[1024,128]{1,0:T(8,128)S(1)} %get-tuple-element.37.t_ref, f32[1024,128]{1,0:T(8,128)S(1)} %get-tuple-element.39.wf_ref, f32[8,128]{1,0:T(8,128)S(1)} %get-tuple-element.40.mass_ref, bf16[256,256]{1,0:T(8,128)(2,1)S(1)} %get-tuple-element.41.dy_ref, ...), custom_call_target="tpu_custom_call" | custom-call | tf_op jit(solution)/shard_map/middle/pallas_call | solution.py:442
  19.9 0.0 collective-permute-done.r0_ref
  19.9 1.7 %collective-permute-done.1.r3_ref = bf16[144,256]{1,0:T(8,128)(2,1)S(1)} collective-permute-done((bf16[144,256]{1,0:T(8,128)(2,1)S(1)}, bf16[144,256]{1,0:T(8,128)(2,1)S(1)}, u32[]{:S(2)}, u32[]{:S(2)}) %collective-permute-start.1) | collective-permute-done | bytes 73760 | tf_op jit(solution)/shard_map/ppermute | solution.py:484
  21.7 0.1 edges.1
  21.8 0.0 copy-start
  21.8 3.4 %early.1 = (f32[1024,128]{1,0:T(8,128)S(1)}, f32[2,128,256]{2,1,0:T(8,128)S(1)}, f32[512,128]{1,0:T(8,128)S(1)}, f32[128,128]{1,0:T(8,128)S(1)}, f32[128,128]{1,...) custom-call(f32[1024,128]{1,0:T(8,128)S(1)} %get-tuple-element.37.t_ref, ...), custom_call_target="tpu_custom_call" | custom-call | tf_op jit(solution)/shard_map/early/pallas_call | solution.py:442
  25.2 0.0 copy-start.1
  25.2 0.0 collective-permute-start.2
  25.2 4.3 %collective-permute-start.3 = (bf16[144,128]{1,0:T(8,128)(2,1)S(1)}, bf16[144,128]{1,0:T(8,128)(2,1)S(1)}, u32[]{:S(2)}, u32[]{:S(2)}) collective-permute-start(bf16[144,128]{1,0:T(8,128)(2,1)S(1)} %get-tuple-element.58.after_ref.to_left_ref), channel_id=1, source_target_pairs={{0,63},{1,0},{2,1},{3,2},{4,3},{5,4},{6,5},{7,6},{8,7},{9,8},{10,9... | collective-permute-start | bytes 110600 | tf_op jit(solution)/shard_map/ppermute | solution.py:462
  29.5 0.0 copy-done
  29.5 0.0 copy-done.1
  29.5 1.3 %winds.1 = (bf16[256,128]{1,0:T(8,128)(2,1)S(1)}, f32[256,128]{1,0:T(8,128)S(1)}, bf16[256,1024]{1,0:T(8,128)(2,1)S(1)}, bf16[1024,256]{1,0:T(8,128)(2,1)S(1)}) custom-call(f32[1024,128]{1,0:T(8,128)S(1)} %get-tuple-element.39.wf_ref, s32[2,128]{1,0:T(2,128)S(1)} %copy-done.1, bf16[256,256]{1,0:T(8,128)(2,1)S(1)} %copy-done, bf16[256,1024]{1,0:T(8,128)(2,1)} %wi_hbm.3, ...), custom_call_target="tpu_custom_call" | custom-call | tf_op jit(solution)/shard_map/winds/pallas_call | solution.py:442
  30.8 0.4 %collective-permute-done.2.cl_ref = bf16[144,128]{1,0:T(8,128)(2,1)S(1)} collective-permute-done((bf16[144,128]{1,0:T(8,128)(2,1)S(1)}, bf16[144,128]{1,0:T(8,128)(2,1)S(1)}, u32[]{:S(2)}, u32[]{:S(2)}) %collective-permute-start.2) | collective-permute-done | bytes 36896 | tf_op jit(solution)/shard_map/ppermute | solution.py:462
  31.1 0.0 collective-permute-done.3.cr_ref
  31.2 2.3 %finish.1 = (f32[1024,128]{1,0:T(8,128)}, bf16[512,128]{1,0:T(8,128)(2,1)}) custom-call(f32[1024,128]{1,0:T(8,128)S(1)} %get-tuple-element.37.t_ref, f32[2,128,256]{2,1,0:T(8,128)S(1)} %get-tuple-element.38.ends_ref, f32[2,128,256]{2,1,0:T(8,128)S(1)} %get-tuple-element.43.middle_ref, f32[4,256]{1,0:T(4,128)S(1)} %get-tuple-element.42.gm_ref, ...), custom_call_target="tpu_custom_call" | custom-call | tf_op jit(solution)/shard_map/finish/pallas_call | solution.py:442
Async XLA Ops:
  2.3 17.6 %collective-permute-start = (bf16[144,256]{1,0:T(8,128)(2,1)S(1)}, bf16[144,256]{1,0:T(8,128)(2,1)S(1)}, u32[]{:S(2)}, u32[]{:S(2)}) collective-permute-start(bf16[144,256]{1,0:T(8,128)(2,1)S(1)} %get-tuple-element.44), channel_id=1, source_target_pairs={{0,960},{64,128},{128,64},{192,256},{256,192},{320,384},{384,320},... | collective-permute-start | bytes 221192 | tf_op jit(solution)/shard_map/ppermute | solution.py:483
  5.7 15.9 %collective-permute-start.1 = (bf16[144,256]{1,0:T(8,128)(2,1)S(1)}, bf16[144,256]{1,0:T(8,128)(2,1)S(1)}, u32[]{:S(2)}, u32[]{:S(2)}) collective-permute-start(bf16[144,256]{1,0:T(8,128)(2,1)S(1)} %get-tuple-element.45), channel_id=1, source_target_pairs={{0,64},{64,0},{128,192},{192,128},{256,320},{320,256},{384,448},{4... | collective-permute-start | bytes 221192 | tf_op jit(solution)/shard_map/ppermute | solution.py:484
  21.8 7.7 %copy-start = (bf16[256,256]{1,0:T(8,128)(2,1)S(1)}, bf16[256,256]{1,0:T(8,128)(2,1)}, u32[]{:S(2)}) copy-start(bf16[256,256]{1,0:T(8,128)(2,1)} %constant.5.clone.rt_hbm.rt_ref) | copy-start | bytes 393220
  25.2 4.4 %copy-start.1 = (s32[2,128]{1,0:T(2,128)S(1)}, s32[2,128]{1,0:T(2,128)}, u32[]{:S(2)}) copy-start(s32[2,128]{1,0:T(2,128)} %cost_ref.1) | copy-start | bytes 3076
  25.2 6.0 %collective-permute-start.2 = (bf16[144,128]{1,0:T(8,128)(2,1)S(1)}, bf16[144,128]{1,0:T(8,128)(2,1)S(1)}, u32[]{:S(2)}, u32[]{:S(2)}) collective-permute-start(bf16[144,128]{1,0:T(8,128)(2,1)S(1)} %get-tuple-element.57.to_right_ref), channel_id=1, source_target_pairs={{0,1},{1,2},{2,3},{3,4},{4,5},{5,6},{6,7},{7,8},{8,9},{9,10},{10,1... | collective-permute-start | bytes 110600 | tf_op jit(solution)/shard_map/ppermute | solution.py:462
  25.2 5.9 %collective-permute-start.3 = (bf16[144,128]{1,0:T(8,128)(2,1)S(1)}, bf16[144,128]{1,0:T(8,128)(2,1)S(1)}, u32[]{:S(2)}, u32[]{:S(2)}) collective-permute-start(bf16[144,128]{1,0:T(8,128)(2,1)S(1)} %get-tuple-element.58.after_ref.to_left_ref), channel_id=1, source_target_pairs={{0,63},{1,0},{2,1},{3,2},{4,3},{5,4},{6,5},{7,6},{8,7},{9,8},{10,9... | collective-permute-start | bytes 110600 | tf_op jit(solution)/shard_map/ppermute | solution.py:462

commit v4 on v3

--- a/solution.py
+++ b/solution.py
@@ -138,18 +138,20 @@
     ]
     for copy in copies:
         copy.start()
-    for copy in copies:
-        copy.wait()
+    copies[2].wait()
     mass = m_ref[...]
     backward = jnp.concatenate([mass[i : i + 1] for i in (3, 2, 1, 0, 7, 6, 5, 4)], axis=0)
     mass = jnp.where(lax.axis_index("grp") % 2 == 1, backward, mass)
     mass_ref[...] = mass
-    wf_ref[...] = w_ref[...].astype(f32)
     mass_rows = assemble_lanes(jnp.concatenate([mass[0:4], mass[4:8]], axis=1))
     gm_ref[...] = mass_rows
     pad = jnp.zeros((ROWS - 129, 256), f32)
     outer_ref[128:, :] = jnp.concatenate([mass_rows[0:1], pad], axis=0).astype(bf16)
     inner_ref[128:, :] = jnp.concatenate([mass_rows[3:4], pad], axis=0).astype(bf16)
+    copies[0].wait()
+    wf_ref[...] = w_ref[...].astype(f32)
+    copies[1].wait()
+    copies[3].wait()
     for channel in range(0, 128, CHUNK):
         rows = slice(channel, channel + CHUNK)
         planes = weighted_rows((0, 3), channel, t_ref, wf_ref, mass, dy_ref)
@@ -244,7 +246,7 @@
 
 def works_early():
     me, last = lax.axis_index("grp"), lax.axis_size("grp") - 1
-    return jnp.logical_and(lax.axis_index("bal") == 0, jnp.logical_and(me != 0, me != last))
+    return jnp.logical_and(lax.axis_index("bal") == 0, jnp.logical_and(me > 0, me < last - 1))
 
 
 def move_tracers(t_ref, ends_ref, middle_ref, gm_ref, r0_ref, r3_ref, columns, t_out, planes_ref, edges=None):

time: 33.6 us -> 33.6 us (level)
  no operation moved by 1% of the time
where the time goes in v4:
time: 33.6 us; the launch traced here: 33.4 us
  starting transfers between devices  21.3 us (63%)
  Pallas kernels  9.2 us (27%)
  waiting for transfers between devices  2.11 us (6%)
  between operations  0.72 us (2%)
    ppermute x1, starting transfers between devices, shards(): r3 = lax.ppermute(inner, 'grp', [(i, i ^ 1) for i in range(count)])  13.6 us
    pallas_call x6, Pallas kernels, run(): pl.pallas_call(kernel, out_shape=shapes, in_specs=[spec(i in hbm_in) for...  9.2 us
    ppermute x2, starting transfers between devices, shift(): lax.ppermute(value, axis, [(i, (i + by) % count) for i in range(count)])  4.33 us
    ppermute x1, starting transfers between devices, shards(): lax.ppermute(outer, 'grp', [(i, (i + (1 if i % 2 else -1)) % count) for i...  3.4 us
    ppermute x1, waiting for transfers between devices, shards(): r3 = lax.ppermute(inner, 'grp', [(i, i ^ 1) for i in range(count)])  1.74 us
  transfers between devices with their start and end apart: 4, of which 2 were waited for; matrix products, arithmetic and copies ran while one was open for 0% of the time, Pallas kernels for 5%

profile of v4, /device:TPU:2, one launch (start us, length us, event | category | flops | bytes accessed | tf_op | source)
XLA Modules:
  0.0 33.4 jit_solution(3753350532536986260)
XLA Ops:
  0.6 1.7 %tendency.1 = (f32[1024,128]{1,0:T(8,128)S(1)}, f32[1024,128]{1,0:T(8,128)S(1)}, f32[8,128]{1,0:T(8,128)S(1)}, bf16[256,256]{1,0:T(8,128)(2,1)S(1)}, f32[2,128,2...) custom-call(f32[1024,128]{1,0:T(8,128)} %bitcast.21, ...), custom_call_target="tpu_custom_call" | custom-call | tf_op jit(solution)/shard_map/tendency/pallas_call | solution.py:444
  2.3 3.4 %collective-permute-start = (bf16[144,256]{1,0:T(8,128)(2,1)S(1)}, bf16[144,256]{1,0:T(8,128)(2,1)S(1)}, u32[]{:S(2)}, u32[]{:S(2)}) collective-permute-start(bf16[144,256]{1,0:T(8,128)(2,1)S(1)} %get-tuple-element.44), channel_id=1, source_target_pairs={{0,960},{64,128},{128,64},{192,256},{256,192},{320,384},{384,320},... | collective-permute-start | bytes 221192 | tf_op jit(solution)/shard_map/ppermute | solution.py:485
  5.7 13.6 %collective-permute-start.1 = (bf16[144,256]{1,0:T(8,128)(2,1)S(1)}, bf16[144,256]{1,0:T(8,128)(2,1)S(1)}, u32[]{:S(2)}, u32[]{:S(2)}) collective-permute-start(bf16[144,256]{1,0:T(8,128)(2,1)S(1)} %get-tuple-element.45), channel_id=1, source_target_pairs={{0,64},{64,0},{128,192},{192,128},{256,320},{320,256},{384,448},{4... | collective-permute-start | bytes 221192 | tf_op jit(solution)/shard_map/ppermute | solution.py:486
  19.3 0.6 %middle.1 = (f32[2,128,256]{2,1,0:T(8,128)S(1)}, f32[144,128]{1,0:T(8,128)S(1)}, f32[144,128]{1,0:T(8,128)S(1)}) custom-call(f32[1024,128]{1,0:T(8,128)S(1)} %get-tuple-element.37.t_ref, f32[1024,128]{1,0:T(8,128)S(1)} %get-tuple-element.39.wf_ref, f32[8,128]{1,0:T(8,128)S(1)} %get-tuple-element.40.mass_ref, bf16[256,256]{1,0:T(8,128)(2,1)S(1)} %get-tuple-element.41.dy_ref, ...), custom_call_target="tpu_custom_call" | custom-call | tf_op jit(solution)/shard_map/middle/pallas_call | solution.py:444
  19.9 0.0 collective-permute-done.r0_ref
  19.9 1.7 %collective-permute-done.1.r3_ref = bf16[144,256]{1,0:T(8,128)(2,1)S(1)} collective-permute-done((bf16[144,256]{1,0:T(8,128)(2,1)S(1)}, bf16[144,256]{1,0:T(8,128)(2,1)S(1)}, u32[]{:S(2)}, u32[]{:S(2)}) %collective-permute-start.1) | collective-permute-done | bytes 73760 | tf_op jit(solution)/shard_map/ppermute | solution.py:486
  21.7 0.1 edges.1
  21.8 0.0 copy-start
  21.8 3.4 %early.1 = (f32[1024,128]{1,0:T(8,128)S(1)}, f32[2,128,256]{2,1,0:T(8,128)S(1)}, f32[512,128]{1,0:T(8,128)S(1)}, f32[128,128]{1,0:T(8,128)S(1)}, f32[128,128]{1,...) custom-call(f32[1024,128]{1,0:T(8,128)S(1)} %get-tuple-element.37.t_ref, ...), custom_call_target="tpu_custom_call" | custom-call | tf_op jit(solution)/shard_map/early/pallas_call | solution.py:444
  25.1 0.0 copy-start.1
  25.2 0.0 collective-permute-start.2
  25.2 4.3 %collective-permute-start.3 = (bf16[144,128]{1,0:T(8,128)(2,1)S(1)}, bf16[144,128]{1,0:T(8,128)(2,1)S(1)}, u32[]{:S(2)}, u32[]{:S(2)}) collective-permute-start(bf16[144,128]{1,0:T(8,128)(2,1)S(1)} %get-tuple-element.58.after_ref.to_left_ref), channel_id=1, source_target_pairs={{0,63},{1,0},{2,1},{3,2},{4,3},{5,4},{6,5},{7,6},{8,7},{9,8},{10,9... | collective-permute-start | bytes 110600 | tf_op jit(solution)/shard_map/ppermute | solution.py:464
  29.5 0.0 copy-done
  29.5 0.0 copy-done.1
  29.5 1.3 %winds.1 = (bf16[256,128]{1,0:T(8,128)(2,1)S(1)}, f32[256,128]{1,0:T(8,128)S(1)}, bf16[256,1024]{1,0:T(8,128)(2,1)S(1)}, bf16[1024,256]{1,0:T(8,128)(2,1)S(1)}) custom-call(f32[1024,128]{1,0:T(8,128)S(1)} %get-tuple-element.39.wf_ref, s32[2,128]{1,0:T(2,128)S(1)} %copy-done.1, bf16[256,256]{1,0:T(8,128)(2,1)S(1)} %copy-done, bf16[256,1024]{1,0:T(8,128)(2,1)} %wi_hbm.3, ...), custom_call_target="tpu_custom_call" | custom-call | tf_op jit(solution)/shard_map/winds/pallas_call | solution.py:444
  30.8 0.4 %collective-permute-done.2.cl_ref = bf16[144,128]{1,0:T(8,128)(2,1)S(1)} collective-permute-done((bf16[144,128]{1,0:T(8,128)(2,1)S(1)}, bf16[144,128]{1,0:T(8,128)(2,1)S(1)}, u32[]{:S(2)}, u32[]{:S(2)}) %collective-permute-start.2) | collective-permute-done | bytes 36896 | tf_op jit(solution)/shard_map/ppermute | solution.py:464
  31.1 0.0 collective-permute-done.3.cr_ref
  31.1 2.3 %finish.1 = (f32[1024,128]{1,0:T(8,128)}, bf16[512,128]{1,0:T(8,128)(2,1)}) custom-call(f32[1024,128]{1,0:T(8,128)S(1)} %get-tuple-element.37.t_ref, f32[2,128,256]{2,1,0:T(8,128)S(1)} %get-tuple-element.38.ends_ref, f32[2,128,256]{2,1,0:T(8,128)S(1)} %get-tuple-element.43.middle_ref, f32[4,256]{1,0:T(4,128)S(1)} %get-tuple-element.42.gm_ref, ...), custom_call_target="tpu_custom_call" | custom-call | tf_op jit(solution)/shard_map/finish/pallas_call | solution.py:444
Async XLA Ops:
  2.3 17.6 %collective-permute-start = (bf16[144,256]{1,0:T(8,128)(2,1)S(1)}, bf16[144,256]{1,0:T(8,128)(2,1)S(1)}, u32[]{:S(2)}, u32[]{:S(2)}) collective-permute-start(bf16[144,256]{1,0:T(8,128)(2,1)S(1)} %get-tuple-element.44), channel_id=1, source_target_pairs={{0,960},{64,128},{128,64},{192,256},{256,192},{320,384},{384,320},... | collective-permute-start | bytes 221192 | tf_op jit(solution)/shard_map/ppermute | solution.py:485
  5.7 15.9 %collective-permute-start.1 = (bf16[144,256]{1,0:T(8,128)(2,1)S(1)}, bf16[144,256]{1,0:T(8,128)(2,1)S(1)}, u32[]{:S(2)}, u32[]{:S(2)}) collective-permute-start(bf16[144,256]{1,0:T(8,128)(2,1)S(1)} %get-tuple-element.45), channel_id=1, source_target_pairs={{0,64},{64,0},{128,192},{192,128},{256,320},{320,256},{384,448},{4... | collective-permute-start | bytes 221192 | tf_op jit(solution)/shard_map/ppermute | solution.py:486
  21.8 7.7 %copy-start = (bf16[256,256]{1,0:T(8,128)(2,1)S(1)}, bf16[256,256]{1,0:T(8,128)(2,1)}, u32[]{:S(2)}) copy-start(bf16[256,256]{1,0:T(8,128)(2,1)} %constant.5.clone.rt_hbm.rt_ref) | copy-start | bytes 393220
  25.1 4.4 %copy-start.1 = (s32[2,128]{1,0:T(2,128)S(1)}, s32[2,128]{1,0:T(2,128)}, u32[]{:S(2)}) copy-start(s32[2,128]{1,0:T(2,128)} %cost_ref.1) | copy-start | bytes 3076
  25.2 6.0 %collective-permute-start.2 = (bf16[144,128]{1,0:T(8,128)(2,1)S(1)}, bf16[144,128]{1,0:T(8,128)(2,1)S(1)}, u32[]{:S(2)}, u32[]{:S(2)}) collective-permute-start(bf16[144,128]{1,0:T(8,128)(2,1)S(1)} %get-tuple-element.57.to_right_ref), channel_id=1, source_target_pairs={{0,1},{1,2},{2,3},{3,4},{4,5},{5,6},{6,7},{7,8},{8,9},{9,10},{10,1... | collective-permute-start | bytes 110600 | tf_op jit(solution)/shard_map/ppermute | solution.py:464
  25.2 5.9 %collective-permute-start.3 = (bf16[144,128]{1,0:T(8,128)(2,1)S(1)}, bf16[144,128]{1,0:T(8,128)(2,1)S(1)}, u32[]{:S(2)}, u32[]{:S(2)}) collective-permute-start(bf16[144,128]{1,0:T(8,128)(2,1)S(1)} %get-tuple-element.58.after_ref.to_left_ref), channel_id=1, source_target_pairs={{0,63},{1,0},{2,1},{3,2},{4,3},{5,4},{6,5},{7,6},{8,7},{9,8},{10,9... | collective-permute-start | bytes 110600 | tf_op jit(solution)/shard_map/ppermute | solution.py:464
